TPU v7x, 128 devices: a whole 4x4x4 slice. The times are simulated.
128 devices in a mesh: outer: 8 (over x, core), inner: 16 (over z, y).
Axes of the slice: x: 4, y: 4, z: 4, core: 2. Of those that a mesh axis runs over, the one named last changes fastest.
Arguments:
- query_in: bfloat16 [16384, 2048], P(('outer', 'inner')), may hold values from -5 to 5
- key_in: bfloat16 [16384, 2048], P(('outer', 'inner')), may hold values from -5 to 5
- value_in: bfloat16 [16384, 2048], P(('outer', 'inner')), may hold values from -384 to 384
- w_out: bfloat16 [2048, 2048], replicated, may hold values from -0.125 to 0.125
- cotangent: bfloat16 [16384, 2048], P(('outer', 'inner')), may hold values from -96 to 96
Outputs:
- output: bfloat16 [16384, 2048], P(('outer', 'inner'))
- query_grad: bfloat16 [16384, 2048], P(('outer', 'inner'))
- key_grad: bfloat16 [16384, 2048], P(('outer', 'inner'))
- value_grad: bfloat16 [16384, 2048], P(('outer', 'inner'))
- w_out_grad: float32 [2048, 2048], P(('outer', 'inner'))
All inputs are finite; a program needn't handle non-finite values.
Results may differ from a plain program's by a relative error of at most 0.035.
Values may be sent and summed in bfloat16 or wider, within the bound.
No kernel may reach another device: no remote copies, remote signals or barrier semaphores. Data moves between devices by JAX's collectives and lax.ppermute only.
A program may use at most 128 MiB of HBM per device.

v0:
```python
import functools
import math

import jax
import jax.numpy as jnp
from jax import lax
from jax.experimental import pallas as pl
from jax.experimental.pallas import tpu as pltpu
from jax.sharding import PartitionSpec as P

HEADS = 16
BLOCK = 128
LEVELS = 3
WIDTH = 128
BF16 = jnp.bfloat16
F32 = jnp.float32
CHUNK = 256
PAIRS = 4


def nt(a, b):
    return lax.dot_general(a, b, (((1,), (1,)), ((), ())), preferred_element_type=F32)


def nn(a, b):
    return lax.dot_general(a, b, (((1,), (0,)), ((), ())), preferred_element_type=F32)


def tn(a, b):
    return lax.dot_general(a, b, (((0,), (0,)), ((), ())), preferred_element_type=F32)


def wide(stat, columns=WIDTH):
    return jnp.broadcast_to(stat, (stat.shape[0], columns))


def evens(ref, base, rows):
    return ref[pl.ds(base, rows, stride=2), :]


def odds(ref, base, rows):
    return ref[pl.ds(base + 1, rows, stride=2), :]


def put_twice(ref, base, value):
    rows = value.shape[0]
    ref[pl.ds(base, rows, stride=2), :] = value
    ref[pl.ds(base + 1, rows, stride=2), :] = value


def across(stat, columns):
    return jnp.concatenate([stat] * (columns // WIDTH), axis=1)


def coarse_blocks(tokens):
    spans, _ = level_rows(tokens)
    out = []
    for height in range(LEVELS, 0, -1):
        base, rows = spans[height]
        for row in range(0, rows, BLOCK):
            near, far = base + row, base + (row ^ BLOCK)
            out.append((height, row, slice(near, near + BLOCK), slice(far, far + BLOCK)))
    return out


def rows_of(token_ref, coarse_ref, x, at):
    tokens = token_ref.shape[0] * BLOCK
    if at.start >= tokens:
        return coarse_ref[x, at.start - tokens : at.stop - tokens, :]
    some = slice(at.start // BLOCK, at.stop // BLOCK)
    return token_ref[some, x * BLOCK : (x + 1) * BLOCK, :].reshape(at.stop - at.start, WIDTH)


def level_rows(tokens):
    out, base = [], 0
    for height in range(LEVELS + 1):
        out.append((base, tokens >> height))
        base += tokens >> height
    return out, base


def kernel_call(body, outs, in_places, mib, scratch=(), cost=None, name=None, after=(), aliases=None):
    count = len(in_places)
    in_places = list(in_places) + ["hbm"] * len(after)

    def ordered(*refs):
        body(*refs[:count], *refs[len(in_places) :])

    spec = {
        "vmem": pl.BlockSpec(memory_space=pltpu.VMEM),
        "hbm": pl.BlockSpec(memory_space=pl.ANY),
    }
    shapes = [
        pltpu.HBM(shape, dtype) if place == "hbm" else jax.ShapeDtypeStruct(shape, dtype)
        for shape, dtype, place in outs
    ]
    call = pl.pallas_call(
        ordered,
        out_shape=shapes,
        in_specs=[spec[place] for place in in_places],
        out_specs=[spec[place] for _, _, place in outs],
        scratch_shapes=list(scratch),
        compiler_params=pltpu.CompilerParams(vmem_limit_bytes=int(mib * 2**20)),
        cost_estimate=cost,
        name=name,
        input_output_aliases=aliases or {},
    )

    def run(*operands):
        operands = [
            pltpu.with_memory_space_constraint(x, pltpu.HBM) if place == "hbm" else x
            for x, place in zip((*operands, *after), in_places)
        ]
        return call(*operands)

    return run


def dma(count):
    return pltpu.SemaphoreType.DMA((count,))


def cost(flops, nbytes):
    return pl.CostEstimate(flops=int(flops), bytes_accessed=int(nbytes), transcendentals=0)


def pack_body(q_ref, k_ref, v_ref, out_ref, held, packed, in_sems, out_sems):
    loads = [
        pltpu.make_async_copy(ref, held.at[x], in_sems.at[x])
        for x, ref in enumerate((q_ref, k_ref, v_ref))
    ]
    for load in loads:
        load.start()
    stores = []
    for x, load in enumerate(loads):
        load.wait()
        rows = slice(x * BLOCK, (x + 1) * BLOCK)
        for h in range(HEADS):
            packed[h, rows, :] = held[x, :, h * WIDTH : (h + 1) * WIDTH]
        stores.append(
            pltpu.make_async_copy(packed.at[:, rows, :], out_ref.at[:, rows, :], out_sems.at[x])
        )
        stores[-1].start()
    for store in stores:
        store.wait()


def pack(q, k, v):
    packed = (HEADS, 3 * BLOCK, WIDTH)
    return kernel_call(
        pack_body,
        [(packed, BF16, "hbm")],
        ["hbm"] * 3,
        6,
        scratch=[pltpu.VMEM((3,) + q.shape, BF16), pltpu.VMEM(packed, BF16), dma(3), dma(3)],
        cost=cost(0, 6 * q.size * 2),
        name="pack_qkv",
    )(q, k, v)[0]


def att_grad_body(chunks, cot_ref, w_ref, out_ref, held, sems):
    rows = held.shape[0] // chunks
    copies = []
    for c in range(chunks):
        at = slice(c * rows, (c + 1) * rows)
        copies.append(pltpu.make_async_copy(w_ref.at[at, :], held.at[at, :], sems.at[c]))
        copies[-1].start()
    for c, copy in enumerate(copies):
        at = slice(c * rows, (c + 1) * rows)
        copy.wait()
        out_ref[:, at] = nt(cot_ref[...], held[at, :]).astype(BF16)


def attended_gradient(cot, w_out):
    chunks = 4
    return kernel_call(
        functools.partial(att_grad_body, chunks),
        [(cot.shape, BF16, "vmem")],
        ["vmem", "hbm"],
        63.6,
        scratch=[pltpu.VMEM(w_out.shape, BF16), dma(chunks)],
        cost=cost(0, 1 << 20),
        name="attended_gradient",
    )(cot, w_out)[0]


def forward_body(
    blocks, qkv_in, grad_in, sent_out, lse_out, lev_out,
    in_ref, grad_ref, out_ref, lse_ref, lev_ref, fq, mu, du, nu, sems,
):
    tokens = blocks * BLOCK
    spans, _ = level_rows(tokens)
    copies, count = [], [0]

    def send(source, target):
        copies.append(pltpu.make_async_copy(source, target, sems.at[count[0]]))
        copies[-1].start()
        count[0] += 1

    scale = 1.0 / math.sqrt(WIDTH)
    parts = 4
    for p in range(parts):
        some = slice(p * blocks // parts, (p + 1) * blocks // parts)
        send(qkv_in.at[some, :, :], in_ref.at[some, :, :])
    send(grad_in, grad_ref)
    loads, copies[:] = copies[:], []
    for b in range(blocks):
        if b % (blocks // parts) == 0:
            loads[b // (blocks // parts)].wait()
        for x in range(3):
            part = in_ref[b, x * BLOCK : (x + 1) * BLOCK, :]
            fq[x, b * BLOCK : (b + 1) * BLOCK, :] = part.astype(F32)
    for height in range(1, LEVELS + 1):
        below, _ = spans[height - 1]
        base, rows = spans[height]
        step = min(CHUNK, rows)
        for x in range(3):
            for r in range(0, rows, step):
                mean = (
                    evens(fq.at[x], below + 2 * r, step) + odds(fq.at[x], below + 2 * r, step)
                ) * 0.5
                mean = mean.astype(BF16)
                lev_ref[x, base - tokens + r : base - tokens + r + step, :] = mean
                fq[x, base + r : base + r + step, :] = mean.astype(F32)

    send(lev_ref, lev_out)

    level = functools.partial(rows_of, in_ref, lev_ref)

    def attend(jobs):
        scores = [nt(level(0, q), level(1, k)) * scale for q, k, _ in jobs]
        tops = [wide(jnp.max(x, axis=1, keepdims=True)) for x in scores]
        expos = [jnp.exp(x - across(top, x.shape[1])) for x, top in zip(scores, tops)]
        numers = [nn(x.astype(BF16), level(2, k)) for x, (_, k, _) in zip(expos, jobs)]
        denoms = [wide(jnp.sum(x, axis=1, keepdims=True)) for x in expos]
        return [
            (top, denom * factor, numer * factor) if factor != 1 else (top, denom, numer)
            for top, denom, numer, (_, _, factor) in zip(tops, denoms, numers, jobs)
        ]

    def merge(at, stats):
        top, denom, numer = stats
        up = mu[at, :]
        peak = jnp.maximum(top, up)
        mine, theirs = jnp.exp(top - peak), jnp.exp(up - peak)
        return peak, mine * denom + theirs * du[at, :], mine * numer + theirs * nu[at, :]

    coarse = coarse_blocks(tokens)
    stats = attend([(near, far, float(2**height)) for height, _, near, far in coarse])
    for (height, row, near, _), one in zip(coarse, stats):
        if height < LEVELS:
            one = merge(near, one)
        for ref, value in zip((mu, du, nu), one):
            put_twice(ref, spans[height - 1][0] + 2 * row, value)
    loads[parts].wait()
    for b in range(blocks):
        out_ref[b, :BLOCK, :] = grad_ref[:, b * WIDTH : (b + 1) * WIDTH]
    for first in range(0, tokens, PAIRS * 2 * BLOCK):
        pairs = [
            slice(row, row + 2 * BLOCK)
            for row in range(first, min(first + PAIRS * 2 * BLOCK, tokens), 2 * BLOCK)
        ]
        for at, one in zip(pairs, attend([(at, at, 1) for at in pairs])):
            peak, total, summed = merge(at, one)
            attended = (summed / total).astype(BF16)
            lse_ref[at, :] = peak + jnp.log(total)
            pair = slice(at.start // BLOCK, at.stop // BLOCK)
            out_ref[pair, BLOCK:, :] = attended.reshape(2, BLOCK, WIDTH)
            send(lse_ref.at[at, :], lse_out.at[at, :])
            send(out_ref.at[pair, :, :], sent_out.at[pair, :, :])
    for copy in copies:
        copy.wait()


def forward(qkv, att_grad, after=()):
    blocks = qkv.shape[0]
    tokens = blocks * BLOCK
    spans, total_rows = level_rows(tokens)
    finer = total_rows - spans[LEVELS][1]
    outs = [
        ((blocks, 2 * BLOCK, WIDTH), BF16, "hbm"),
        ((tokens, WIDTH), F32, "hbm"),
        ((3, total_rows - tokens, WIDTH), BF16, "hbm"),
    ]
    return kernel_call(
        functools.partial(forward_body, blocks),
        outs,
        ["hbm"] * 2,
        32,
        scratch=[
            pltpu.VMEM(qkv.shape, BF16),
            pltpu.VMEM(att_grad.shape, BF16),
            pltpu.VMEM((blocks, 2 * BLOCK, WIDTH), BF16),
            pltpu.VMEM((tokens, WIDTH), F32),
            pltpu.VMEM((3, total_rows - tokens, WIDTH), BF16),
            pltpu.VMEM((3, total_rows, WIDTH), F32),
            pltpu.VMEM((finer, WIDTH), F32),
            pltpu.VMEM((finer, WIDTH), F32),
            pltpu.VMEM((finer, WIDTH), F32),
            dma(6 + blocks),
        ],
        cost=cost(4 * tokens * 384 * WIDTH, 8 << 20),
        name="head_forward",
        after=after,
    )(qkv, att_grad)


def backward_body(
    blocks, grad_in, sent_in, lse_in, lev_in, qkv_in, rows_in, w_in, grads_out, output_ref,
    out_ref, att_ref, lev_ref, qkv_ref, ys, ds, rs, cg, up, rows_ref, w_ref, sems,
):
    tokens = blocks * BLOCK
    spans, _ = level_rows(tokens)
    scale = 1.0 / math.sqrt(WIDTH)
    parts, count = 4, [0]

    def fetch(source, target):
        copy = pltpu.make_async_copy(source, target, sems.at[count[0]])
        count[0] += 1
        copy.start()
        return copy

    first_loads = []
    for p in range(parts):
        some = slice(p * blocks // parts, (p + 1) * blocks // parts)
        at = slice(p * tokens // parts, (p + 1) * tokens // parts)
        first_loads.append(
            [
                fetch(grad_in.at[at, :], cg.at[at, :]),
                fetch(sent_in.at[some, BLOCK:, :], att_ref.at[some, :, :]),
                fetch(lse_in.at[at, :], rs.at[at, :]),
            ]
        )
    later_loads = [
        fetch(lev_in, lev_ref),
        fetch(qkv_in, qkv_ref),
        fetch(rows_in, rows_ref),
        fetch(w_in, w_ref),
    ]
    for b in range(blocks):
        if b % (blocks // parts) == 0:
            for copy in first_loads[b // (blocks // parts)]:
                copy.wait()
        at = slice(b * BLOCK, (b + 1) * BLOCK)
        grad = cg[at, :].astype(F32)
        ys[at, :] = grad
        ds[at, :] = wide(jnp.sum(grad * att_ref[b].astype(F32), axis=1, keepdims=True))
    for height in range(1, LEVELS + 1):
        below, _ = spans[height - 1]
        base, rows = spans[height]
        for r in range(0, rows, BLOCK):
            at = slice(base + r, base + r + BLOCK)
            first = below + 2 * r
            lo, hi = evens(rs, first, BLOCK), odds(rs, first, BLOCK)
            low = jnp.minimum(lo, hi)
            lo, hi = jnp.exp(low - lo), jnp.exp(low - hi)
            grad = lo * evens(ys, first, BLOCK) + hi * odds(ys, first, BLOCK)
            delta = lo * evens(ds, first, BLOCK) + hi * odds(ds, first, BLOCK)
            ys[at, :], ds[at, :], rs[at, :] = grad, delta, low
            cg[at, :] = grad.astype(BF16)

    level = functools.partial(rows_of, qkv_ref, lev_ref)

    def gradients(jobs):
        scores = [nt(level(0, q), level(1, k)) * scale for q, k in jobs]
        inner = [nt(cg[q, :], level(2, k)) for q, k in jobs]
        expos = [
            jnp.exp(x - across(rs[q, :], x.shape[1])) for x, (q, _) in zip(scores, jobs)
        ]
        sgrads = [
            (expo * (x - across(ds[q, :], x.shape[1])) * scale).astype(BF16)
            for expo, x, (q, _) in zip(expos, inner, jobs)
        ]
        probs = [expo.astype(BF16) for expo in expos]
        q_parts = [nn(x, level(1, k)) for x, (_, k) in zip(sgrads, jobs)]
        k_parts = [tn(x, level(0, q)) for x, (q, _) in zip(sgrads, jobs)]
        v_parts = [tn(x, cg[q, :]) for x, (q, _) in zip(probs, jobs)]
        return list(zip(q_parts, k_parts, v_parts))

    later_loads[0].wait()
    coarse = coarse_blocks(tokens)
    for (height, row, near, far), parts in zip(
        coarse, gradients([(near, far) for _, _, near, far in coarse])
    ):
        for x, (at, first) in enumerate(((near, row), (far, row ^ BLOCK), (far, row ^ BLOCK))):
            value = parts[x]
            if height < LEVELS:
                value = value + up[x, at, :]
            put_twice(up.at[x], spans[height - 1][0] + 2 * first, value)
    later_loads[1].wait()
    stores = []
    for first in range(0, tokens, PAIRS * 2 * BLOCK):
        pairs = [
            slice(row, row + 2 * BLOCK)
            for row in range(first, min(first + PAIRS * 2 * BLOCK, tokens), 2 * BLOCK)
        ]
        for at, parts in zip(pairs, gradients([(at, at) for at in pairs])):
            pair = slice(at.start // BLOCK, at.stop // BLOCK)
            for x, value in enumerate(parts):
                value = (value + up[x, at, :]).astype(BF16)
                out_ref[pair, x * BLOCK : (x + 1) * BLOCK, :] = value.reshape(2, BLOCK, WIDTH)
            stores.append(fetch(out_ref.at[pair, :, :], grads_out.at[pair, : 3 * BLOCK, :]))
    later_loads[2].wait()
    later_loads[3].wait()
    rows = jnp.concatenate([rows_ref[h] for h in range(HEADS)], axis=1)
    width = w_ref.shape[1]
    for first in range(0, width, 512):
        at = slice(first, first + 512)
        output_ref[:, at] = nn(rows, w_ref[:, at]).astype(BF16)
    for store in stores:
        store.wait()


def backward(grad, sent, lse, lev, qkv, rows, w_out, after):
    blocks = sent.shape[0]
    tokens = blocks * BLOCK
    spans, total_rows = level_rows(tokens)
    finer = total_rows - spans[LEVELS][1]
    extra = w_out.size // lax.axis_size("outer") // blocks // WIDTH
    return kernel_call(
        functools.partial(backward_body, blocks),
        [
            ((blocks, 3 * BLOCK + extra, WIDTH), BF16, "hbm"),
            ((BLOCK, w_out.shape[1]), BF16, "vmem"),
        ],
        ["hbm"] * 7,
        63.6,
        scratch=[
            pltpu.VMEM((blocks, 3 * BLOCK, WIDTH), BF16),
            pltpu.VMEM(rows.shape, BF16),
            pltpu.VMEM(lev.shape, BF16),
            pltpu.VMEM(qkv.shape, BF16),
            pltpu.VMEM((total_rows, WIDTH), F32),
            pltpu.VMEM((total_rows, WIDTH), F32),
            pltpu.VMEM((total_rows, WIDTH), F32),
            pltpu.VMEM((total_rows, WIDTH), BF16),
            pltpu.VMEM((3, finer, WIDTH), F32),
            pltpu.VMEM(rows.shape, BF16),
            pltpu.VMEM(w_out.shape, BF16),
            dma(16 + blocks // 2),
        ],
        cost=cost(10 * tokens * 384 * WIDTH + 2 * BLOCK * w_out.size, 24 << 20),
        name="head_backward",
        after=after,
    )(grad.reshape(tokens, WIDTH), sent, lse, lev, qkv, rows, w_out)


def tile_body(groups, per, _, att_in, *refs):
    cot_refs = refs[:groups]
    out_ref, att_ref, lhs, held, tile, sems = refs[groups:]
    chunk = lhs.shape[0] // HEADS
    chunks, step = held.shape[0], held.shape[2]
    att_copy = pltpu.make_async_copy(att_in, att_ref, sems.at[0])
    att_copy.start()
    copies, stores = [], []
    for c in range(chunks):
        for k, ref in enumerate(cot_refs):
            copies.append(
                pltpu.make_async_copy(
                    ref.at[:, c * step : (c + 1) * step],
                    held.at[c, k * BLOCK : (k + 1) * BLOCK, :],
                    sems.at[1 + c * groups + k],
                )
            )
            copies[-1].start()
    att_copy.wait()
    mine = lax.axis_index("outer")
    for k in range(groups):
        for j in range(per):
            lhs[j * WIDTH : (j + 1) * WIDTH, k * BLOCK : (k + 1) * BLOCK] = att_ref[
                (mine ^ k) * per + j
            ].T
    for c in range(chunks):
        for copy in copies[c * groups : (c + 1) * groups]:
            copy.wait()
        part = nn(lhs[...], held[c]).astype(BF16)
        first = c * step
        for i in range(HEADS):
            for j in range(step // WIDTH):
                to = (first // WIDTH + j) * chunk
                tile[i, to : to + chunk, :] = part[
                    i * chunk : (i + 1) * chunk, j * WIDTH : (j + 1) * WIDTH
                ]
        done = slice(first // WIDTH * chunk, (first + step) // WIDTH * chunk)
        to = slice(3 * BLOCK + done.start, 3 * BLOCK + done.stop)
        stores.append(
            pltpu.make_async_copy(
                tile.at[:, done, :], out_ref.at[:, to, :], sems.at[1 + chunks * groups + c]
            )
        )
        stores[-1].start()
    for store in stores:
        store.wait()


def with_tile(grads, att, pieces):
    groups, width = len(pieces), pieces[0].shape[1]
    per = HEADS // groups
    chunk = per * WIDTH // HEADS
    extra = chunk * (width // WIDTH)
    chunks = 4
    return kernel_call(
        functools.partial(tile_body, groups, per),
        [(grads.shape, BF16, "hbm")],
        ["hbm"] * (2 + groups),
        18,
        scratch=[
            pltpu.VMEM(att.shape, BF16),
            pltpu.VMEM((per * WIDTH, groups * BLOCK), BF16),
            pltpu.VMEM((chunks, groups * BLOCK, width // chunks), BF16),
            pltpu.VMEM((HEADS, extra, WIDTH), BF16),
            dma(1 + chunks * (groups + 1)),
        ],
        aliases={0: 0},
        cost=cost(2 * groups * BLOCK * per * WIDTH * width, 10 << 20),
        name="projection_tile",
    )(grads, att, *pieces)[0]


def unpack_body(scale, in_ref, q_out, k_out, v_out, w_out, grads, w_ref, sems):
    chunk, width = w_ref.shape
    stores = []

    def send(source, target):
        stores.append(pltpu.make_async_copy(source, target, sems.at[len(stores)]))
        stores[-1].start()

    for x, target in enumerate((q_out, k_out, v_out)):
        for h in range(HEADS):
            grads[x, :, h * WIDTH : (h + 1) * WIDTH] = in_ref[h, x * BLOCK : (x + 1) * BLOCK, :]
        send(grads.at[x], target)
    for c in range(width // WIDTH):
        at = 3 * BLOCK + c * chunk
        total = in_ref[0, at : at + chunk, :].astype(F32)
        for h in range(1, HEADS):
            total = total + in_ref[h, at : at + chunk, :].astype(F32)
        w_ref[:, c * WIDTH : (c + 1) * WIDTH] = total * scale
    send(w_ref, w_out)
    for store in stores:
        store.wait()


def unpack(got, scale):
    chunk = (got.shape[1] - 3 * BLOCK) // HEADS
    width = HEADS * WIDTH
    return kernel_call(
        functools.partial(unpack_body, scale),
        [((BLOCK, width), BF16, "hbm")] * 3 + [((chunk, width), F32, "hbm")],
        ["vmem"],
        8,
        scratch=[
            pltpu.VMEM((3, BLOCK, width), BF16),
            pltpu.VMEM((chunk, width), F32),
            dma(4),
        ],
        cost=cost(0, 6 << 20),
        name="unpack_grads",
    )(got)


def split_body(got_ref, grad_ref, att_ref, sems):
    copies = [
        pltpu.make_async_copy(got_ref.at[:, BLOCK:, :], att_ref, sems.at[0]),
        pltpu.make_async_copy(got_ref.at[:, :BLOCK, :], grad_ref, sems.at[1]),
    ]
    for copy in copies:
        copy.start()
    for copy in copies:
        copy.wait()


def split(got):
    return kernel_call(
        split_body,
        [((HEADS, BLOCK, WIDTH), BF16, "hbm")] * 2,
        ["vmem"],
        2,
        scratch=[dma(2)],
        cost=cost(0, 2 << 20),
        name="split_attended",
    )(got)


def swap(value, axis):
    return lax.all_to_all(value, axis, 0, 0, tiled=True)


def from_outer(value, apart):
    size = lax.axis_size("outer")
    return lax.ppermute(value, "outer", [(i, i ^ apart) for i in range(size)])


def on_device(query_in, key_in, value_in, w_out, cotangent):
    groups = lax.axis_size("outer")
    tokens = query_in.shape[0] * lax.axis_size(("outer", "inner"))
    pieces = {k: from_outer(cotangent, k) if k else cotangent for k in range(groups) if k < 2 or k & 3 == 2}
    soon = [pieces[k] for k in pieces if k]
    qkv = swap(pack(query_in, key_in, value_in), "inner")
    att_grad = attended_gradient(cotangent, w_out)
    sent, lse, lev = forward(qkv, att_grad, after=soon)
    late = {k: from_outer(pieces[k + 2], 2) for k in range(4, groups, 4)}
    pieces.update(late)
    for k in range(2, groups, 2):
        pieces[k + 1] = from_outer(pieces[k], 1)
    grad, att = split(swap(sent, "inner"))
    att_outer = swap(att, "outer")
    grads, output = backward(grad, sent, lse, lev, qkv, att, w_out, list(late.values()))
    pieces = [pieces[k] for k in range(groups)]
    last = swap(with_tile(grads, att_outer, pieces), "inner")
    query_grad, key_grad, value_grad, w_out_grad = unpack(last, 1.0 / math.sqrt(tokens))
    return output, query_grad, key_grad, value_grad, w_out_grad


def solution(mesh):
    rows = P(("outer", "inner"), None)
    return jax.shard_map(
        on_device,
        mesh=mesh,
        in_specs=(rows, rows, rows, P(), rows),
        out_specs=(rows,) * 5,
        check_vma=False,
    )
```

profile of v0, /device:TPU:0, one launch (start us, length us, event | category | flops | bytes accessed | tf_op | source)
XLA Modules:
  0.0 120.8 jit_solution(13629990812424737516)
XLA Ops:
  0.6 2.4 %pack_qkv.1 = bf16[16,384,128]{2,1,0:T(8,128)(2,1)} custom-call(bf16[128,2048]{1,0:T(8,128)(2,1)} %refs_0_.2, bf16[128,2048]{1,0:T(8,128)(2,1)} %refs_1_.2, bf16[128,2048]{1,0:T(8,128)(2,1)} %refs_2_.2), custom_call_target="tpu_custom_call" | custom-call | bytes 3145728 | tf_op jit(solution)/shard_map/pack_qkv/pallas_call | solution.py:114
  3.0 8.2 %all-to-all-start = ((bf16[16,384,128]{2,1,0:T(8,128)(2,1)}), bf16[16,384,128]{2,1,0:T(8,128)(2,1)}, u32[]{:S(2)}, u32[]{:S(2)}) async-start(bf16[16,384,128]{2,1,0:T(8,128)(2,1)} %pack_qkv.1), calls=%async_computation | async-start | bytes 3145728 | tf_op jit(solution)/shard_map/all_to_all | solution.py:585
  11.2 2.8 %collective-permute-start.2 = (bf16[128,2048]{1,0:T(8,128)(2,1)}, bf16[128,2048]{1,0:T(8,128)(2,1)}, u32[]{:S(2)}, u32[]{:S(2)}) collective-permute-start(bf16[128,2048]{1,0:T(8,128)(2,1)} %refs_2_.3), channel_id=1, source_target_pairs={{0,96},{16,112},{32,64},{48,80},{64,32},{80,48},{96,0},{112,16},{1... | collective-permute-start | bytes 1572872 | tf_op jit(solution)/shard_map/ppermute | solution.py:590
  14.0 0.2 collective-permute-start.1
  14.3 0.0 collective-permute-start
  14.3 6.8 %attended_gradient.1.refs_1_ = bf16[128,2048]{1,0:T(8,128)(2,1)} custom-call(bf16[128,2048]{1,0:T(8,128)(2,1)} %refs_2_.3, bf16[2048,2048]{1,0:T(8,128)(2,1)} %refs_6_.1), custom_call_target="tpu_custom_call" | custom-call | bytes 1048576 | tf_op jit(solution)/shard_map/attended_gradient/pallas_call | solution.py:114
  21.1 5.1 %collective-permute-done.2.refs_4_.refs_8_ = bf16[128,2048]{1,0:T(8,128)(2,1)} collective-permute-done((bf16[128,2048]{1,0:T(8,128)(2,1)}, bf16[128,2048]{1,0:T(8,128)(2,1)}, u32[]{:S(2)}, u32[]{:S(2)}) %collective-permute-start.2) | collective-permute-done | bytes 524320 | tf_op jit(solution)/shard_map/ppermute | solution.py:590
  26.2 1.3 %collective-permute-done.1.refs_3_.refs_4_ = bf16[128,2048]{1,0:T(8,128)(2,1)} collective-permute-done((bf16[128,2048]{1,0:T(8,128)(2,1)}, bf16[128,2048]{1,0:T(8,128)(2,1)}, u32[]{:S(2)}, u32[]{:S(2)}) %collective-permute-start.1) | collective-permute-done | bytes 524320 | tf_op jit(solution)/shard_map/ppermute | solution.py:590
  27.5 0.0 collective-permute-done.refs_2_.refs_3_
  27.5 8.3 %all-to-all-done.refs_0_.refs_4_ = bf16[16,384,128]{2,1,0:T(8,128)(2,1)} async-done(((bf16[16,384,128]{2,1,0:T(8,128)(2,1)}), bf16[16,384,128]{2,1,0:T(8,128)(2,1)}, u32[]{:S(2)}, u32[]{:S(2)}) %all-to-all-start) | async-done | bytes 1572896 | tf_op jit(solution)/shard_map/all_to_all | solution.py:585
  35.7 5.4 %head_forward.1 = (bf16[16,256,128]{2,1,0:T(8,128)(2,1)}, f32[2048,128]{1,0:T(8,128)}, bf16[3,1792,128]{2,1,0:T(8,128)(2,1)}) custom-call(bf16[16,384,128]{2,1,0:T(8,128)(2,1)} %all-to-all-done.refs_0_.refs_4_, bf16[128,2048]{1,0:T(8,128)(2,1)} %attended_gradient.1.refs_1_, bf16[128,2048]{1,0:T(8,128)(2,1)} %collective-permute-done.refs_2_.refs_3_, ...), custom_call_target="tpu_custom_call" | custom-call | flops 402653184 | bytes 8388608 | tf_op jit(solution)/shard_map/head_forward/pallas_call | solution.py:114
  41.2 3.7 %all-to-all-start.1 = ((bf16[16,256,128]{2,1,0:T(8,128)(2,1)}), bf16[16,256,128]{2,1,0:T(8,128)(2,1)S(1)}, u32[]{:S(2)}, u32[]{:S(2)}) async-start(bf16[16,256,128]{2,1,0:T(8,128)(2,1)} %get-tuple-element.16.refs_1_), calls=%async_computation.1 | async-start | bytes 2097152 | tf_op jit(solution)/shard_map/all_to_all | solution.py:585
  44.8 1.6 %collective-permute-start.3 = (bf16[128,2048]{1,0:T(8,128)(2,1)}, bf16[128,2048]{1,0:T(8,128)(2,1)}, u32[]{:S(2)}, u32[]{:S(2)}) collective-permute-start(bf16[128,2048]{1,0:T(8,128)(2,1)} %collective-permute-done.2.refs_4_.refs_8_), channel_id=1, source_target_pairs={{0,32},{16,48},{32,0},{48,16},{64,96},{80,112},{96,64},{112,80},{1... | collective-permute-start | bytes 1572872 | tf_op jit(solution)/shard_map/ppermute | solution.py:590
  46.4 0.0 collective-permute-start.6
  46.4 0.5 collective-permute-start.4
  46.9 11.0 %collective-permute-done.3.refs_7_.refs_6_ = bf16[128,2048]{1,0:T(8,128)(2,1)} collective-permute-done((bf16[128,2048]{1,0:T(8,128)(2,1)}, bf16[128,2048]{1,0:T(8,128)(2,1)}, u32[]{:S(2)}, u32[]{:S(2)}) %collective-permute-start.3) | collective-permute-done | bytes 524320 | tf_op jit(solution)/shard_map/ppermute | solution.py:590
  57.9 0.0 collective-permute-start.5
  57.9 3.7 %all-to-all-done.1.refs_0_ = bf16[16,256,128]{2,1,0:T(8,128)(2,1)S(1)} async-done(((bf16[16,256,128]{2,1,0:T(8,128)(2,1)}), bf16[16,256,128]{2,1,0:T(8,128)(2,1)S(1)}, u32[]{:S(2)}, u32[]{:S(2)}) %all-to-all-start.1) | async-done | bytes 1048608 | tf_op jit(solution)/shard_map/all_to_all | solution.py:585
  61.6 1.0 split_attended.1
  62.6 4.3 %all-to-all-start.2 = ((bf16[16,128,128]{2,1,0:T(8,128)(2,1)}), bf16[16,128,128]{2,1,0:T(8,128)(2,1)}, u32[]{:S(2)}, u32[]{:S(2)}) async-start(bf16[16,128,128]{2,1,0:T(8,128)(2,1)} %get-tuple-element.20.refs_5_), calls=%async_computation.2 | async-start | bytes 1048576 | tf_op jit(solution)/shard_map/all_to_all | solution.py:585
  66.9 7.6 %head_backward.1 = (bf16[16,640,128]{2,1,0:T(8,128)(2,1)}, bf16[128,2048]{1,0:T(8,128)(2,1)}) custom-call(bf16[2048,128]{1,0:T(8,128)(2,1)} %bitcast.1, bf16[16,256,128]{2,1,0:T(8,128)(2,1)} %get-tuple-element.16.refs_1_, f32[2048,128]{1,0:T(8,128)} %get-tuple-element.18.refs_2_, bf16[3,1792,128]{2,1,0:T(8,128)(2,1)} %get-tuple-element.19.refs_3_, ...), custom_call_target="tpu_custom_call" | custom-call | flops 2080374784 | bytes 25165824 | tf_op jit(solution)/shard_map/head_backward/pallas_call | solution.py:114
  74.6 0.0 collective-permute-done.6.refs_9_
  74.6 0.0 collective-permute-done.4.refs_5_
  74.6 0.0 collective-permute-done.5.refs_7_
  74.6 2.7 %all-to-all-done.2.refs_1_ = bf16[16,128,128]{2,1,0:T(8,128)(2,1)} async-done(((bf16[16,128,128]{2,1,0:T(8,128)(2,1)}), bf16[16,128,128]{2,1,0:T(8,128)(2,1)}, u32[]{:S(2)}, u32[]{:S(2)}) %all-to-all-start.2) | async-done | bytes 524320 | tf_op jit(solution)/shard_map/all_to_all | solution.py:585
  77.3 4.2 %projection_tile.1 = bf16[16,640,128]{2,1,0:T(8,128)(2,1)} custom-call(bf16[16,640,128]{2,1,0:T(8,128)(2,1)} %get-tuple-element.22.refs_0_, bf16[16,128,128]{2,1,0:T(8,128)(2,1)} %all-to-all-done.2.refs_1_, bf16[128,2048]{1,0:T(8,128)(2,1)} %refs_2_.3, bf16[128,2048]{1,0:T(8,128)(2,1)} %collective-permute-done.refs_2_.refs_3_, ...), custom_call_target="tpu_custom_call", output_to_operand_aliasing={{}: (0, {})} | custom-call | flops 1073741824 | bytes 10485760 | tf_op jit(solution)/shard_map/projection_tile/pallas_call | solution.py:114
  81.5 37.8 %all_to_all.20.refs_0_ = bf16[16,640,128]{2,1,0:T(8,128)(2,1)S(1)} all-to-all(bf16[16,640,128]{2,1,0:T(8,128)(2,1)} %projection_tile.1), channel_id=1, replica_groups=mesh['outer'=8,'inner'=16] {'inner'}, dimensions={0} | all-to-all | bytes 5242880 | tf_op jit(solution)/shard_map/all_to_all | solution.py:585
  119.3 1.3 %unpack_grads.1 = (bf16[128,2048]{1,0:T(8,128)(2,1)}, bf16[128,2048]{1,0:T(8,128)(2,1)}, bf16[128,2048]{1,0:T(8,128)(2,1)}, f32[16,2048]{1,0:T(8,128)}) custom-call(bf16[16,640,128]{2,1,0:T(8,128)(2,1)S(1)} %all_to_all.20.refs_0_), custom_call_target="tpu_custom_call" | custom-call | bytes 6291456 | tf_op jit(solution)/shard_map/unpack_grads/pallas_call | solution.py:114
Async XLA Ops:
  3.0 32.7 %all-to-all-start = ((bf16[16,384,128]{2,1,0:T(8,128)(2,1)}), bf16[16,384,128]{2,1,0:T(8,128)(2,1)}, u32[]{:S(2)}, u32[]{:S(2)}) async-start(bf16[16,384,128]{2,1,0:T(8,128)(2,1)} %pack_qkv.1), calls=%async_computation | async-start | bytes 3145728 | tf_op jit(solution)/shard_map/all_to_all | solution.py:585
  11.2 15.0 %collective-permute-start.2 = (bf16[128,2048]{1,0:T(8,128)(2,1)}, bf16[128,2048]{1,0:T(8,128)(2,1)}, u32[]{:S(2)}, u32[]{:S(2)}) collective-permute-start(bf16[128,2048]{1,0:T(8,128)(2,1)} %refs_2_.3), channel_id=1, source_target_pairs={{0,96},{16,112},{32,64},{48,80},{64,32},{80,48},{96,0},{112,16},{1... | collective-permute-start | bytes 1572872 | tf_op jit(solution)/shard_map/ppermute | solution.py:590
  14.0 13.4 %collective-permute-start.1 = (bf16[128,2048]{1,0:T(8,128)(2,1)}, bf16[128,2048]{1,0:T(8,128)(2,1)}, u32[]{:S(2)}, u32[]{:S(2)}) collective-permute-start(bf16[128,2048]{1,0:T(8,128)(2,1)} %refs_2_.3), channel_id=1, source_target_pairs={{0,32},{16,48},{32,0},{48,16},{64,96},{80,112},{96,64},{112,80},{1... | collective-permute-start | bytes 1572872 | tf_op jit(solution)/shard_map/ppermute | solution.py:590
  14.3 13.2 %collective-permute-start = (bf16[128,2048]{1,0:T(8,128)(2,1)}, bf16[128,2048]{1,0:T(8,128)(2,1)}, u32[]{:S(2)}, u32[]{:S(2)}) collective-permute-start(bf16[128,2048]{1,0:T(8,128)(2,1)} %refs_2_.3), channel_id=1, source_target_pairs={{0,16},{16,0},{32,48},{48,32},{64,80},{80,64},{96,112},{112,96},{1... | collective-permute-start | bytes 1572872 | tf_op jit(solution)/shard_map/ppermute | solution.py:590
  41.2 20.4 %all-to-all-start.1 = ((bf16[16,256,128]{2,1,0:T(8,128)(2,1)}), bf16[16,256,128]{2,1,0:T(8,128)(2,1)S(1)}, u32[]{:S(2)}, u32[]{:S(2)}) async-start(bf16[16,256,128]{2,1,0:T(8,128)(2,1)} %get-tuple-element.16.refs_1_), calls=%async_computation.1 | async-start | bytes 2097152 | tf_op jit(solution)/shard_map/all_to_all | solution.py:585
  44.8 13.1 %collective-permute-start.3 = (bf16[128,2048]{1,0:T(8,128)(2,1)}, bf16[128,2048]{1,0:T(8,128)(2,1)}, u32[]{:S(2)}, u32[]{:S(2)}) collective-permute-start(bf16[128,2048]{1,0:T(8,128)(2,1)} %collective-permute-done.2.refs_4_.refs_8_), channel_id=1, source_target_pairs={{0,32},{16,48},{32,0},{48,16},{64,96},{80,112},{96,64},{112,80},{1... | collective-permute-start | bytes 1572872 | tf_op jit(solution)/shard_map/ppermute | solution.py:590
  46.4 28.2 %collective-permute-start.6 = (bf16[128,2048]{1,0:T(8,128)(2,1)}, bf16[128,2048]{1,0:T(8,128)(2,1)}, u32[]{:S(2)}, u32[]{:S(2)}) collective-permute-start(bf16[128,2048]{1,0:T(8,128)(2,1)} %collective-permute-done.2.refs_4_.refs_8_), channel_id=1, source_target_pairs={{0,16},{16,0},{32,48},{48,32},{64,80},{80,64},{96,112},{112,96},{1... | collective-permute-start | bytes 1572872 | tf_op jit(solution)/shard_map/ppermute | solution.py:590
  46.4 28.2 %collective-permute-start.4 = (bf16[128,2048]{1,0:T(8,128)(2,1)}, bf16[128,2048]{1,0:T(8,128)(2,1)}, u32[]{:S(2)}, u32[]{:S(2)}) collective-permute-start(bf16[128,2048]{1,0:T(8,128)(2,1)} %collective-permute-done.1.refs_3_.refs_4_), channel_id=1, source_target_pairs={{0,16},{16,0},{32,48},{48,32},{64,80},{80,64},{96,112},{112,96},{1... | collective-permute-start | bytes 1572872 | tf_op jit(solution)/shard_map/ppermute | solution.py:590
  57.9 16.6 %collective-permute-start.5 = (bf16[128,2048]{1,0:T(8,128)(2,1)}, bf16[128,2048]{1,0:T(8,128)(2,1)}, u32[]{:S(2)}, u32[]{:S(2)}) collective-permute-start(bf16[128,2048]{1,0:T(8,128)(2,1)} %collective-permute-done.3.refs_7_.refs_6_), channel_id=1, source_target_pairs={{0,16},{16,0},{32,48},{48,32},{64,80},{80,64},{96,112},{112,96},{1... | collective-permute-start | bytes 1572872 | tf_op jit(solution)/shard_map/ppermute | solution.py:590
  62.6 14.8 %all-to-all-start.2 = ((bf16[16,128,128]{2,1,0:T(8,128)(2,1)}), bf16[16,128,128]{2,1,0:T(8,128)(2,1)}, u32[]{:S(2)}, u32[]{:S(2)}) async-start(bf16[16,128,128]{2,1,0:T(8,128)(2,1)} %get-tuple-element.20.refs_5_), calls=%async_computation.2 | async-start | bytes 1048576 | tf_op jit(solution)/shard_map/all_to_all | solution.py:585
where the time goes:
time: 121 us
  blocking collectives  37.8 us (31%)
  waiting for transfers between devices  32.1 us (27%)
  Pallas kernels  28.7 us (24%)
  starting transfers between devices  21.3 us (18%)
    all_to_all x1, blocking collectives, swap(): return lax.all_to_all(value, axis, 0, 0, tiled=True)  37.8 us
    pallas_call x7, Pallas kernels, run(): return call(*operands)  28.7 us
    ppermute x7, waiting for transfers between devices, from_outer(): return lax.ppermute(value, 'outer', [(i, i ^ apart) for i in range(size)])  17.4 us
    all_to_all x3, starting transfers between devices, swap(): return lax.all_to_all(value, axis, 0, 0, tiled=True)  16.2 us
    all_to_all x3, waiting for transfers between devices, swap(): return lax.all_to_all(value, axis, 0, 0, tiled=True)  14.7 us
    ppermute x7, starting transfers between devices, from_outer(): return lax.ppermute(value, 'outer', [(i, i ^ apart) for i in range(size)])  5.15 us
  transfers between devices with their start and end apart: 10, of which 6 were waited for; matrix products, arithmetic and copies ran while one was open for 0% of the time, Pallas kernels for 13%

commit v1 on v0

--- a/solution.py
+++ b/solution.py
@@ -46,6 +46,12 @@
     rows = value.shape[0]
     ref[pl.ds(base, rows, stride=2), :] = value
     ref[pl.ds(base + 1, rows, stride=2), :] = value
+
+
+def diagonal(matrix):
+    rows = lax.broadcasted_iota(jnp.int32, matrix.shape, 0)
+    columns = lax.broadcasted_iota(jnp.int32, matrix.shape, 1)
+    return jnp.where(rows == columns, matrix, 0.0)
 
 
 def across(stat, columns):
@@ -255,6 +261,7 @@
     loads[parts].wait()
     for b in range(blocks):
         out_ref[b, :BLOCK, :] = grad_ref[:, b * WIDTH : (b + 1) * WIDTH]
+    send(out_ref.at[:, :BLOCK, :], sent_out.at[:, :BLOCK, :])
     for first in range(0, tokens, PAIRS * 2 * BLOCK):
         pairs = [
             slice(row, row + 2 * BLOCK)
@@ -263,11 +270,15 @@
         for at, one in zip(pairs, attend([(at, at, 1) for at in pairs])):
             peak, total, summed = merge(at, one)
             attended = (summed / total).astype(BF16)
-            lse_ref[at, :] = peak + jnp.log(total)
+            lse = peak + jnp.log(total)
+            for half in range(2):
+                b = at.start // BLOCK + half
+                part = lse[half * BLOCK : (half + 1) * BLOCK]
+                lse_ref[b : b + 1, :] = jnp.sum(diagonal(part), axis=0, keepdims=True)
             pair = slice(at.start // BLOCK, at.stop // BLOCK)
             out_ref[pair, BLOCK:, :] = attended.reshape(2, BLOCK, WIDTH)
-            send(lse_ref.at[at, :], lse_out.at[at, :])
-            send(out_ref.at[pair, :, :], sent_out.at[pair, :, :])
+            send(out_ref.at[pair, BLOCK:, :], sent_out.at[pair, BLOCK:, :])
+    send(lse_ref, lse_out)
     for copy in copies:
         copy.wait()
 
@@ -279,7 +290,7 @@
     finer = total_rows - spans[LEVELS][1]
     outs = [
         ((blocks, 2 * BLOCK, WIDTH), BF16, "hbm"),
-        ((tokens, WIDTH), F32, "hbm"),
+        ((blocks, BLOCK), F32, "hbm"),
         ((3, total_rows - tokens, WIDTH), BF16, "hbm"),
     ]
     return kernel_call(
@@ -291,13 +302,13 @@
             pltpu.VMEM(qkv.shape, BF16),
             pltpu.VMEM(att_grad.shape, BF16),
             pltpu.VMEM((blocks, 2 * BLOCK, WIDTH), BF16),
-            pltpu.VMEM((tokens, WIDTH), F32),
+            pltpu.VMEM((blocks, BLOCK), F32),
             pltpu.VMEM((3, total_rows - tokens, WIDTH), BF16),
             pltpu.VMEM((3, total_rows, WIDTH), F32),
             pltpu.VMEM((finer, WIDTH), F32),
             pltpu.VMEM((finer, WIDTH), F32),
             pltpu.VMEM((finer, WIDTH), F32),
-            dma(6 + blocks),
+            dma(8 + blocks // 2),
         ],
         cost=cost(4 * tokens * 384 * WIDTH, 8 << 20),
         name="head_forward",
@@ -307,7 +318,7 @@
 
 def backward_body(
     blocks, grad_in, sent_in, lse_in, lev_in, qkv_in, rows_in, w_in, grads_out, output_ref,
-    out_ref, att_ref, lev_ref, qkv_ref, ys, ds, rs, cg, up, rows_ref, w_ref, sems,
+    out_ref, att_ref, lse_ref, lev_ref, qkv_ref, ys, ds, rs, cg, up, rows_ref, w_ref, sems,
 ):
     tokens = blocks * BLOCK
     spans, _ = level_rows(tokens)
@@ -321,6 +332,7 @@
         return copy
 
     first_loads = []
+    lse_load = fetch(lse_in, lse_ref)
     for p in range(parts):
         some = slice(p * blocks // parts, (p + 1) * blocks // parts)
         at = slice(p * tokens // parts, (p + 1) * tokens // parts)
@@ -328,7 +340,6 @@
             [
                 fetch(grad_in.at[at, :], cg.at[at, :]),
                 fetch(sent_in.at[some, BLOCK:, :], att_ref.at[some, :, :]),
-                fetch(lse_in.at[at, :], rs.at[at, :]),
             ]
         )
     later_loads = [
@@ -337,11 +348,14 @@
         fetch(rows_in, rows_ref),
         fetch(w_in, w_ref),
     ]
+    lse_load.wait()
     for b in range(blocks):
         if b % (blocks // parts) == 0:
             for copy in first_loads[b // (blocks // parts)]:
                 copy.wait()
         at = slice(b * BLOCK, (b + 1) * BLOCK)
+        lse = jnp.broadcast_to(lse_ref[b : b + 1, :], (BLOCK, BLOCK))
+        rs[at, :] = wide(jnp.sum(diagonal(lse), axis=1, keepdims=True))
         grad = cg[at, :].astype(F32)
         ys[at, :] = grad
         ds[at, :] = wide(jnp.sum(grad * att_ref[b].astype(F32), axis=1, keepdims=True))
@@ -428,6 +442,7 @@
         scratch=[
             pltpu.VMEM((blocks, 3 * BLOCK, WIDTH), BF16),
             pltpu.VMEM(rows.shape, BF16),
+            pltpu.VMEM(lse.shape, F32),
             pltpu.VMEM(lev.shape, BF16),
             pltpu.VMEM(qkv.shape, BF16),
             pltpu.VMEM((total_rows, WIDTH), F32),

time: 121 us -> 121 us (level)
  no operation moved by 1% of the time
where the time goes in v1:
time: 121 us
  blocking collectives  37.8 us (31%)
  waiting for transfers between devices  32.3 us (27%)
  Pallas kernels  28.3 us (23%)
  starting transfers between devices  21.3 us (18%)
    all_to_all x1, blocking collectives, swap(): return lax.all_to_all(value, axis, 0, 0, tiled=True)  37.8 us
    pallas_call x7, Pallas kernels, run(): return call(*operands)  28.3 us
    ppermute x7, waiting for transfers between devices, from_outer(): return lax.ppermute(value, 'outer', [(i, i ^ apart) for i in range(size)])  17.4 us
    all_to_all x3, starting transfers between devices, swap(): return lax.all_to_all(value, axis, 0, 0, tiled=True)  16.2 us
    all_to_all x3, waiting for transfers between devices, swap(): return lax.all_to_all(value, axis, 0, 0, tiled=True)  14.8 us
    ppermute x7, starting transfers between devices, from_outer(): return lax.ppermute(value, 'outer', [(i, i ^ apart) for i in range(size)])  5.15 us
  transfers between devices with their start and end apart: 10, of which 6 were waited for; matrix products, arithmetic and copies ran while one was open for 0% of the time, Pallas kernels for 13%

profile of v1, /device:TPU:0, one launch (start us, length us, event | category | flops | bytes accessed | tf_op | source)
XLA Modules:
  0.0 120.5 jit_solution(3190651235285705299)
XLA Ops:
  0.6 2.4 %pack_qkv.1 = bf16[16,384,128]{2,1,0:T(8,128)(2,1)} custom-call(bf16[128,2048]{1,0:T(8,128)(2,1)} %refs_0_.2, bf16[128,2048]{1,0:T(8,128)(2,1)} %refs_1_.2, bf16[128,2048]{1,0:T(8,128)(2,1)} %refs_2_.2), custom_call_target="tpu_custom_call" | custom-call | bytes 3145728 | tf_op jit(solution)/shard_map/pack_qkv/pallas_call | solution.py:120
  3.0 8.2 %all-to-all-start = ((bf16[16,384,128]{2,1,0:T(8,128)(2,1)}), bf16[16,384,128]{2,1,0:T(8,128)(2,1)}, u32[]{:S(2)}, u32[]{:S(2)}) async-start(bf16[16,384,128]{2,1,0:T(8,128)(2,1)} %pack_qkv.1), calls=%async_computation | async-start | bytes 3145728 | tf_op jit(solution)/shard_map/all_to_all | solution.py:600
  11.2 2.8 %collective-permute-start.2 = (bf16[128,2048]{1,0:T(8,128)(2,1)}, bf16[128,2048]{1,0:T(8,128)(2,1)}, u32[]{:S(2)}, u32[]{:S(2)}) collective-permute-start(bf16[128,2048]{1,0:T(8,128)(2,1)} %refs_2_.3), channel_id=1, source_target_pairs={{0,96},{16,112},{32,64},{48,80},{64,32},{80,48},{96,0},{112,16},{1... | collective-permute-start | bytes 1572872 | tf_op jit(solution)/shard_map/ppermute | solution.py:605
  14.0 0.2 collective-permute-start.1
  14.3 0.0 collective-permute-start
  14.3 6.8 %attended_gradient.1.refs_1_ = bf16[128,2048]{1,0:T(8,128)(2,1)} custom-call(bf16[128,2048]{1,0:T(8,128)(2,1)} %refs_2_.3, bf16[2048,2048]{1,0:T(8,128)(2,1)} %refs_6_.1), custom_call_target="tpu_custom_call" | custom-call | bytes 1048576 | tf_op jit(solution)/shard_map/attended_gradient/pallas_call | solution.py:120
  21.1 5.1 %collective-permute-done.2.refs_4_.refs_8_ = bf16[128,2048]{1,0:T(8,128)(2,1)} collective-permute-done((bf16[128,2048]{1,0:T(8,128)(2,1)}, bf16[128,2048]{1,0:T(8,128)(2,1)}, u32[]{:S(2)}, u32[]{:S(2)}) %collective-permute-start.2) | collective-permute-done | bytes 524320 | tf_op jit(solution)/shard_map/ppermute | solution.py:605
  26.2 1.3 %collective-permute-done.1.refs_3_.refs_4_ = bf16[128,2048]{1,0:T(8,128)(2,1)} collective-permute-done((bf16[128,2048]{1,0:T(8,128)(2,1)}, bf16[128,2048]{1,0:T(8,128)(2,1)}, u32[]{:S(2)}, u32[]{:S(2)}) %collective-permute-start.1) | collective-permute-done | bytes 524320 | tf_op jit(solution)/shard_map/ppermute | solution.py:605
  27.5 0.0 collective-permute-done.refs_2_.refs_3_
  27.5 8.3 %all-to-all-done.refs_0_.refs_4_ = bf16[16,384,128]{2,1,0:T(8,128)(2,1)} async-done(((bf16[16,384,128]{2,1,0:T(8,128)(2,1)}), bf16[16,384,128]{2,1,0:T(8,128)(2,1)}, u32[]{:S(2)}, u32[]{:S(2)}) %all-to-all-start) | async-done | bytes 1572896 | tf_op jit(solution)/shard_map/all_to_all | solution.py:600
  35.7 5.2 %head_forward.1 = (bf16[16,256,128]{2,1,0:T(8,128)(2,1)}, f32[16,128]{1,0:T(8,128)}, bf16[3,1792,128]{2,1,0:T(8,128)(2,1)}) custom-call(bf16[16,384,128]{2,1,0:T(8,128)(2,1)} %all-to-all-done.refs_0_.refs_4_, bf16[128,2048]{1,0:T(8,128)(2,1)} %attended_gradient.1.refs_1_, bf16[128,2048]{1,0:T(8,128)(2,1)} %collective-permute-done.refs_2_.refs_3_, ...), custom_call_target="tpu_custom_call" | custom-call | flops 402653184 | bytes 8388608 | tf_op jit(solution)/shard_map/head_forward/pallas_call | solution.py:120
  40.9 3.7 %all-to-all-start.1 = ((bf16[16,256,128]{2,1,0:T(8,128)(2,1)}), bf16[16,256,128]{2,1,0:T(8,128)(2,1)S(1)}, u32[]{:S(2)}, u32[]{:S(2)}) async-start(bf16[16,256,128]{2,1,0:T(8,128)(2,1)} %get-tuple-element.16.refs_1_), calls=%async_computation.1 | async-start | bytes 2097152 | tf_op jit(solution)/shard_map/all_to_all | solution.py:600
  44.6 1.6 %collective-permute-start.3 = (bf16[128,2048]{1,0:T(8,128)(2,1)}, bf16[128,2048]{1,0:T(8,128)(2,1)}, u32[]{:S(2)}, u32[]{:S(2)}) collective-permute-start(bf16[128,2048]{1,0:T(8,128)(2,1)} %collective-permute-done.2.refs_4_.refs_8_), channel_id=1, source_target_pairs={{0,32},{16,48},{32,0},{48,16},{64,96},{80,112},{96,64},{112,80},{1... | collective-permute-start | bytes 1572872 | tf_op jit(solution)/shard_map/ppermute | solution.py:605
  46.1 0.0 collective-permute-start.6
  46.1 0.5 collective-permute-start.4
  46.7 11.0 %collective-permute-done.3.refs_7_.refs_6_ = bf16[128,2048]{1,0:T(8,128)(2,1)} collective-permute-done((bf16[128,2048]{1,0:T(8,128)(2,1)}, bf16[128,2048]{1,0:T(8,128)(2,1)}, u32[]{:S(2)}, u32[]{:S(2)}) %collective-permute-start.3) | collective-permute-done | bytes 524320 | tf_op jit(solution)/shard_map/ppermute | solution.py:605
  57.7 0.0 collective-permute-start.5
  57.7 3.7 %all-to-all-done.1.refs_0_ = bf16[16,256,128]{2,1,0:T(8,128)(2,1)S(1)} async-done(((bf16[16,256,128]{2,1,0:T(8,128)(2,1)}), bf16[16,256,128]{2,1,0:T(8,128)(2,1)S(1)}, u32[]{:S(2)}, u32[]{:S(2)}) %all-to-all-start.1) | async-done | bytes 1048608 | tf_op jit(solution)/shard_map/all_to_all | solution.py:600
  61.3 1.0 split_attended.1
  62.3 4.3 %all-to-all-start.2 = ((bf16[16,128,128]{2,1,0:T(8,128)(2,1)}), bf16[16,128,128]{2,1,0:T(8,128)(2,1)}, u32[]{:S(2)}, u32[]{:S(2)}) async-start(bf16[16,128,128]{2,1,0:T(8,128)(2,1)} %get-tuple-element.20.refs_5_), calls=%async_computation.2 | async-start | bytes 1048576 | tf_op jit(solution)/shard_map/all_to_all | solution.py:600
  66.7 7.4 %head_backward.1 = (bf16[16,640,128]{2,1,0:T(8,128)(2,1)}, bf16[128,2048]{1,0:T(8,128)(2,1)}) custom-call(bf16[2048,128]{1,0:T(8,128)(2,1)} %bitcast.1, bf16[16,256,128]{2,1,0:T(8,128)(2,1)} %get-tuple-element.16.refs_1_, f32[16,128]{1,0:T(8,128)} %get-tuple-element.18.refs_2_, bf16[3,1792,128]{2,1,0:T(8,128)(2,1)} %get-tuple-element.19.refs_3_, ...), custom_call_target="tpu_custom_call" | custom-call | flops 2080374784 | bytes 25165824 | tf_op jit(solution)/shard_map/head_backward/pallas_call | solution.py:120
  74.1 0.0 collective-permute-done.6.refs_9_
  74.1 0.0 collective-permute-done.4.refs_5_
  74.1 0.0 collective-permute-done.5.refs_7_
  74.2 2.9 %all-to-all-done.2.refs_1_ = bf16[16,128,128]{2,1,0:T(8,128)(2,1)} async-done(((bf16[16,128,128]{2,1,0:T(8,128)(2,1)}), bf16[16,128,128]{2,1,0:T(8,128)(2,1)}, u32[]{:S(2)}, u32[]{:S(2)}) %all-to-all-start.2) | async-done | bytes 524320 | tf_op jit(solution)/shard_map/all_to_all | solution.py:600
  77.1 4.2 %projection_tile.1 = bf16[16,640,128]{2,1,0:T(8,128)(2,1)} custom-call(bf16[16,640,128]{2,1,0:T(8,128)(2,1)} %get-tuple-element.22.refs_0_, bf16[16,128,128]{2,1,0:T(8,128)(2,1)} %all-to-all-done.2.refs_1_, bf16[128,2048]{1,0:T(8,128)(2,1)} %refs_2_.3, bf16[128,2048]{1,0:T(8,128)(2,1)} %collective-permute-done.refs_2_.refs_3_, ...), custom_call_target="tpu_custom_call", output_to_operand_aliasing={{}: (0, {})} | custom-call | flops 1073741824 | bytes 10485760 | tf_op jit(solution)/shard_map/projection_tile/pallas_call | solution.py:120
  81.3 37.8 %all_to_all.20.refs_0_ = bf16[16,640,128]{2,1,0:T(8,128)(2,1)S(1)} all-to-all(bf16[16,640,128]{2,1,0:T(8,128)(2,1)} %projection_tile.1), channel_id=1, replica_groups=mesh['outer'=8,'inner'=16] {'inner'}, dimensions={0} | all-to-all | bytes 5242880 | tf_op jit(solution)/shard_map/all_to_all | solution.py:600
  119.0 1.3 %unpack_grads.1 = (bf16[128,2048]{1,0:T(8,128)(2,1)}, bf16[128,2048]{1,0:T(8,128)(2,1)}, bf16[128,2048]{1,0:T(8,128)(2,1)}, f32[16,2048]{1,0:T(8,128)}) custom-call(bf16[16,640,128]{2,1,0:T(8,128)(2,1)S(1)} %all_to_all.20.refs_0_), custom_call_target="tpu_custom_call" | custom-call | bytes 6291456 | tf_op jit(solution)/shard_map/unpack_grads/pallas_call | solution.py:120
Async XLA Ops:
  3.0 32.7 %all-to-all-start = ((bf16[16,384,128]{2,1,0:T(8,128)(2,1)}), bf16[16,384,128]{2,1,0:T(8,128)(2,1)}, u32[]{:S(2)}, u32[]{:S(2)}) async-start(bf16[16,384,128]{2,1,0:T(8,128)(2,1)} %pack_qkv.1), calls=%async_computation | async-start | bytes 3145728 | tf_op jit(solution)/shard_map/all_to_all | solution.py:600
  11.2 15.0 %collective-permute-start.2 = (bf16[128,2048]{1,0:T(8,128)(2,1)}, bf16[128,2048]{1,0:T(8,128)(2,1)}, u32[]{:S(2)}, u32[]{:S(2)}) collective-permute-start(bf16[128,2048]{1,0:T(8,128)(2,1)} %refs_2_.3), channel_id=1, source_target_pairs={{0,96},{16,112},{32,64},{48,80},{64,32},{80,48},{96,0},{112,16},{1... | collective-permute-start | bytes 1572872 | tf_op jit(solution)/shard_map/ppermute | solution.py:605
  14.0 13.4 %collective-permute-start.1 = (bf16[128,2048]{1,0:T(8,128)(2,1)}, bf16[128,2048]{1,0:T(8,128)(2,1)}, u32[]{:S(2)}, u32[]{:S(2)}) collective-permute-start(bf16[128,2048]{1,0:T(8,128)(2,1)} %refs_2_.3), channel_id=1, source_target_pairs={{0,32},{16,48},{32,0},{48,16},{64,96},{80,112},{96,64},{112,80},{1... | collective-permute-start | bytes 1572872 | tf_op jit(solution)/shard_map/ppermute | solution.py:605
  14.3 13.2 %collective-permute-start = (bf16[128,2048]{1,0:T(8,128)(2,1)}, bf16[128,2048]{1,0:T(8,128)(2,1)}, u32[]{:S(2)}, u32[]{:S(2)}) collective-permute-start(bf16[128,2048]{1,0:T(8,128)(2,1)} %refs_2_.3), channel_id=1, source_target_pairs={{0,16},{16,0},{32,48},{48,32},{64,80},{80,64},{96,112},{112,96},{1... | collective-permute-start | bytes 1572872 | tf_op jit(solution)/shard_map/ppermute | solution.py:605
  40.9 20.4 %all-to-all-start.1 = ((bf16[16,256,128]{2,1,0:T(8,128)(2,1)}), bf16[16,256,128]{2,1,0:T(8,128)(2,1)S(1)}, u32[]{:S(2)}, u32[]{:S(2)}) async-start(bf16[16,256,128]{2,1,0:T(8,128)(2,1)} %get-tuple-element.16.refs_1_), calls=%async_computation.1 | async-start | bytes 2097152 | tf_op jit(solution)/shard_map/all_to_all | solution.py:600
  44.6 13.1 %collective-permute-start.3 = (bf16[128,2048]{1,0:T(8,128)(2,1)}, bf16[128,2048]{1,0:T(8,128)(2,1)}, u32[]{:S(2)}, u32[]{:S(2)}) collective-permute-start(bf16[128,2048]{1,0:T(8,128)(2,1)} %collective-permute-done.2.refs_4_.refs_8_), channel_id=1, source_target_pairs={{0,32},{16,48},{32,0},{48,16},{64,96},{80,112},{96,64},{112,80},{1... | collective-permute-start | bytes 1572872 | tf_op jit(solution)/shard_map/ppermute | solution.py:605
  46.1 28.0 %collective-permute-start.6 = (bf16[128,2048]{1,0:T(8,128)(2,1)}, bf16[128,2048]{1,0:T(8,128)(2,1)}, u32[]{:S(2)}, u32[]{:S(2)}) collective-permute-start(bf16[128,2048]{1,0:T(8,128)(2,1)} %collective-permute-done.2.refs_4_.refs_8_), channel_id=1, source_target_pairs={{0,16},{16,0},{32,48},{48,32},{64,80},{80,64},{96,112},{112,96},{1... | collective-permute-start | bytes 1572872 | tf_op jit(solution)/shard_map/ppermute | solution.py:605
  46.1 28.0 %collective-permute-start.4 = (bf16[128,2048]{1,0:T(8,128)(2,1)}, bf16[128,2048]{1,0:T(8,128)(2,1)}, u32[]{:S(2)}, u32[]{:S(2)}) collective-permute-start(bf16[128,2048]{1,0:T(8,128)(2,1)} %collective-permute-done.1.refs_3_.refs_4_), channel_id=1, source_target_pairs={{0,16},{16,0},{32,48},{48,32},{64,80},{80,64},{96,112},{112,96},{1... | collective-permute-start | bytes 1572872 | tf_op jit(solution)/shard_map/ppermute | solution.py:605
  57.7 16.5 %collective-permute-start.5 = (bf16[128,2048]{1,0:T(8,128)(2,1)}, bf16[128,2048]{1,0:T(8,128)(2,1)}, u32[]{:S(2)}, u32[]{:S(2)}) collective-permute-start(bf16[128,2048]{1,0:T(8,128)(2,1)} %collective-permute-done.3.refs_7_.refs_6_), channel_id=1, source_target_pairs={{0,16},{16,0},{32,48},{48,32},{64,80},{80,64},{96,112},{112,96},{1... | collective-permute-start | bytes 1572872 | tf_op jit(solution)/shard_map/ppermute | solution.py:605
  62.3 14.8 %all-to-all-start.2 = ((bf16[16,128,128]{2,1,0:T(8,128)(2,1)}), bf16[16,128,128]{2,1,0:T(8,128)(2,1)}, u32[]{:S(2)}, u32[]{:S(2)}) async-start(bf16[16,128,128]{2,1,0:T(8,128)(2,1)} %get-tuple-element.20.refs_5_), calls=%async_computation.2 | async-start | bytes 1048576 | tf_op jit(solution)/shard_map/all_to_all | solution.py:600

commit v2 on v1

--- a/solution.py
+++ b/solution.py
@@ -16,6 +16,7 @@
 F32 = jnp.float32
 CHUNK = 256
 PAIRS = 4
+GRAD_CHUNKS = 4
 
 
 def nt(a, b):
@@ -130,13 +131,52 @@
     return pl.CostEstimate(flops=int(flops), bytes_accessed=int(nbytes), transcendentals=0)
 
 
-def pack_body(q_ref, k_ref, v_ref, out_ref, held, packed, in_sems, out_sems):
+def odd_core():
+    return lax.axis_index("outer") & 1 == 1
+
+
+def gradient(cot_ref, w_ref, grad_out, cot, held, grad, sems):
+    rows = held.shape[0] // GRAD_CHUNKS
+    load = pltpu.make_async_copy(cot_ref, cot, sems.at[GRAD_CHUNKS])
+    load.start()
+    copies = []
+    for c in range(GRAD_CHUNKS):
+        at = slice(c * rows, (c + 1) * rows)
+        copies.append(pltpu.make_async_copy(w_ref.at[at, :], held.at[at, :], sems.at[c]))
+        copies[-1].start()
+    load.wait()
+    for c, copy in enumerate(copies):
+        at = slice(c * rows, (c + 1) * rows)
+        copy.wait()
+        grad[:, at] = nt(cot[...], held[at, :]).astype(BF16)
+    store = pltpu.make_async_copy(grad, grad_out, sems.at[GRAD_CHUNKS + 1])
+    store.start()
+    store.wait()
+
+
+def gradient_scratch(cot, w_out):
+    return [
+        pltpu.VMEM(cot.shape, BF16),
+        pltpu.VMEM(w_out.shape, BF16),
+        pltpu.VMEM(cot.shape, BF16),
+        dma(GRAD_CHUNKS + 2),
+    ]
+
+
+def pack_body(
+    q_ref, k_ref, v_ref, cot_ref, w_ref, out_ref, grad_out, held, packed, in_sems, out_sems, *room
+):
     loads = [
         pltpu.make_async_copy(ref, held.at[x], in_sems.at[x])
         for x, ref in enumerate((q_ref, k_ref, v_ref))
     ]
     for load in loads:
         load.start()
+
+    @pl.when(odd_core())
+    def _():
+        gradient(cot_ref, w_ref, grad_out, *room)
+
     stores = []
     for x, load in enumerate(loads):
         load.wait()
@@ -151,43 +191,37 @@
         store.wait()
 
 
-def pack(q, k, v):
+def pack(q, k, v, cot, w_out):
     packed = (HEADS, 3 * BLOCK, WIDTH)
     return kernel_call(
         pack_body,
-        [(packed, BF16, "hbm")],
-        ["hbm"] * 3,
-        6,
-        scratch=[pltpu.VMEM((3,) + q.shape, BF16), pltpu.VMEM(packed, BF16), dma(3), dma(3)],
+        [(packed, BF16, "hbm"), (cot.shape, BF16, "hbm")],
+        ["hbm"] * 5,
+        18,
+        scratch=[pltpu.VMEM((3,) + q.shape, BF16), pltpu.VMEM(packed, BF16), dma(3), dma(3)]
+        + gradient_scratch(cot, w_out),
         cost=cost(0, 6 * q.size * 2),
         name="pack_qkv",
-    )(q, k, v)[0]
-
-
-def att_grad_body(chunks, cot_ref, w_ref, out_ref, held, sems):
-    rows = held.shape[0] // chunks
-    copies = []
-    for c in range(chunks):
-        at = slice(c * rows, (c + 1) * rows)
-        copies.append(pltpu.make_async_copy(w_ref.at[at, :], held.at[at, :], sems.at[c]))
-        copies[-1].start()
-    for c, copy in enumerate(copies):
-        at = slice(c * rows, (c + 1) * rows)
-        copy.wait()
-        out_ref[:, at] = nt(cot_ref[...], held[at, :]).astype(BF16)
-
-
-def attended_gradient(cot, w_out):
-    chunks = 4
+    )(q, k, v, cot, w_out)
+
+
+def late_gradient_body(_, cot_ref, w_ref, grad_out, *room):
+    @pl.when(jnp.logical_not(odd_core()))
+    def _():
+        gradient(cot_ref, w_ref, grad_out, *room)
+
+
+def late_gradient(grad, cot, w_out):
     return kernel_call(
-        functools.partial(att_grad_body, chunks),
-        [(cot.shape, BF16, "vmem")],
-        ["vmem", "hbm"],
+        late_gradient_body,
+        [(grad.shape, BF16, "hbm")],
+        ["hbm"] * 3,
         63.6,
-        scratch=[pltpu.VMEM(w_out.shape, BF16), dma(chunks)],
+        scratch=gradient_scratch(cot, w_out),
         cost=cost(0, 1 << 20),
         name="attended_gradient",
-    )(cot, w_out)[0]
+        aliases={0: 0},
+    )(grad, cot, w_out)[0]
 
 
 def forward_body(
@@ -610,8 +644,9 @@
     tokens = query_in.shape[0] * lax.axis_size(("outer", "inner"))
     pieces = {k: from_outer(cotangent, k) if k else cotangent for k in range(groups) if k < 2 or k & 3 == 2}
     soon = [pieces[k] for k in pieces if k]
-    qkv = swap(pack(query_in, key_in, value_in), "inner")
-    att_grad = attended_gradient(cotangent, w_out)
+    packed, att_grad = pack(query_in, key_in, value_in, cotangent, w_out)
+    qkv = swap(packed, "inner")
+    att_grad = late_gradient(att_grad, cotangent, w_out)
     sent, lse, lev = forward(qkv, att_grad, after=soon)
     late = {k: from_outer(pieces[k + 2], 2) for k in range(4, groups, 4)}
     pieces.update(late)

time: 121 us -> 121 us (level)
  starting transfers between devices: 21.3 us -> 31.3 us
  waiting for transfers between devices: 32.3 us -> 23.5 us
    ppermute x7, starting transfers between devices: 5.15 us -> 11.9 us  [from_outer(): return lax.ppermute(value, 'outer', [(i, i ^ apart) for i in range(size)])]
    ppermute x7, waiting for transfers between devices: 17.4 us -> 11.5 us  [from_outer(): return lax.ppermute(value, 'outer', [(i, i ^ apart) for i in range(size)])]
    all_to_all x3, starting transfers between devices: 16.2 us -> 19.4 us  [swap(): return lax.all_to_all(value, axis, 0, 0, tiled=True)]
    all_to_all x3, waiting for transfers between devices: 14.8 us -> 12 us  [swap(): return lax.all_to_all(value, axis, 0, 0, tiled=True)]
  transfers between devices with their start and end apart: 10 -> 10, of which waited for: 6 -> 5; matrix products, arithmetic and copies ran while one was open for 0% -> 0% of each run, Pallas kernels for 13% -> 12%
where the time goes in v2:
time: 121 us
  blocking collectives  37.8 us (31%)
  starting transfers between devices  31.3 us (26%)
  Pallas kernels  27.4 us (23%)
  waiting for transfers between devices  23.5 us (19%)
    all_to_all x1, blocking collectives, swap(): return lax.all_to_all(value, axis, 0, 0, tiled=True)  37.8 us
    pallas_call x7, Pallas kernels, run(): return call(*operands)  27.4 us
    all_to_all x3, starting transfers between devices, swap(): return lax.all_to_all(value, axis, 0, 0, tiled=True)  19.4 us
    all_to_all x3, waiting for transfers between devices, swap(): return lax.all_to_all(value, axis, 0, 0, tiled=True)  12 us
    ppermute x7, starting transfers between devices, from_outer(): return lax.ppermute(value, 'outer', [(i, i ^ apart) for i in range(size)])  11.9 us
    ppermute x7, waiting for transfers between devices, from_outer(): return lax.ppermute(value, 'outer', [(i, i ^ apart) for i in range(size)])  11.5 us
  transfers between devices with their start and end apart: 10, of which 5 were waited for; matrix products, arithmetic and copies ran while one was open for 0% of the time, Pallas kernels for 12%

profile of v2, /device:TPU:0, one launch (start us, length us, event | category | flops | bytes accessed | tf_op | source)
XLA Modules:
  0.0 120.8 jit_solution(15406726423212562186)
XLA Ops:
  0.6 2.4 %pack_qkv.1 = (bf16[16,384,128]{2,1,0:T(8,128)(2,1)}, bf16[128,2048]{1,0:T(8,128)(2,1)}) custom-call(bf16[128,2048]{1,0:T(8,128)(2,1)} %refs_0_.1, bf16[128,2048]{1,0:T(8,128)(2,1)} %refs_1_.2, bf16[128,2048]{1,0:T(8,128)(2,1)} %refs_2_.3, bf16[128,2048]{1,0:T(8,128)(2,1)} %refs_2_.5, bf16[2048,2048]{1,0:T(8,128)(2,1)} %refs_6_.1), custom_call_target="tpu_custom_call" | custom-call | bytes 3145728 | tf_op jit(solution)/shard_map/pack_qkv/pallas_call | solution.py:121
  3.1 8.2 %all-to-all-start = ((bf16[16,384,128]{2,1,0:T(8,128)(2,1)}), bf16[16,384,128]{2,1,0:T(8,128)(2,1)}, u32[]{:S(2)}, u32[]{:S(2)}) async-start(bf16[16,384,128]{2,1,0:T(8,128)(2,1)} %get-tuple-element.18), calls=%async_computation | async-start | bytes 3145728 | tf_op jit(solution)/shard_map/all_to_all | solution.py:634
  11.3 2.8 %collective-permute-start.2 = (bf16[128,2048]{1,0:T(8,128)(2,1)}, bf16[128,2048]{1,0:T(8,128)(2,1)}, u32[]{:S(2)}, u32[]{:S(2)}) collective-permute-start(bf16[128,2048]{1,0:T(8,128)(2,1)} %refs_2_.5), channel_id=1, source_target_pairs={{0,96},{16,112},{32,64},{48,80},{64,32},{80,48},{96,0},{112,16},{1... | collective-permute-start | bytes 1572872 | tf_op jit(solution)/shard_map/ppermute | solution.py:639
  14.1 0.2 collective-permute-start.1
  14.3 4.4 %collective-permute-start = (bf16[128,2048]{1,0:T(8,128)(2,1)}, bf16[128,2048]{1,0:T(8,128)(2,1)}, u32[]{:S(2)}, u32[]{:S(2)}) collective-permute-start(bf16[128,2048]{1,0:T(8,128)(2,1)} %refs_2_.5), channel_id=1, source_target_pairs={{0,16},{16,0},{32,48},{48,32},{64,80},{80,64},{96,112},{112,96},{1... | collective-permute-start | bytes 1572872 | tf_op jit(solution)/shard_map/ppermute | solution.py:639
  18.7 5.9 %attended_gradient.1.refs_1_ = bf16[128,2048]{1,0:T(8,128)(2,1)} custom-call(bf16[128,2048]{1,0:T(8,128)(2,1)} %get-tuple-element.19.refs_0_, bf16[128,2048]{1,0:T(8,128)(2,1)} %refs_2_.5, bf16[2048,2048]{1,0:T(8,128)(2,1)} %refs_6_.1), custom_call_target="tpu_custom_call", output_to_operand_aliasing={{}: (0, {})} | custom-call | bytes 1048576 | tf_op jit(solution)/shard_map/attended_gradient/pallas_call | solution.py:121
  24.6 0.0 collective-permute-done.2.refs_4_.refs_8_
  24.6 0.9 collective-permute-done.1.refs_3_.refs_4_
  25.5 0.0 collective-permute-done.refs_2_.refs_3_
  25.5 6.5 %all-to-all-done.refs_0_.refs_4_ = bf16[16,384,128]{2,1,0:T(8,128)(2,1)} async-done(((bf16[16,384,128]{2,1,0:T(8,128)(2,1)}), bf16[16,384,128]{2,1,0:T(8,128)(2,1)}, u32[]{:S(2)}, u32[]{:S(2)}) %all-to-all-start) | async-done | bytes 1572896 | tf_op jit(solution)/shard_map/all_to_all | solution.py:634
  32.1 5.2 %head_forward.1 = (bf16[16,256,128]{2,1,0:T(8,128)(2,1)}, f32[16,128]{1,0:T(8,128)}, bf16[3,1792,128]{2,1,0:T(8,128)(2,1)}) custom-call(bf16[16,384,128]{2,1,0:T(8,128)(2,1)} %all-to-all-done.refs_0_.refs_4_, bf16[128,2048]{1,0:T(8,128)(2,1)} %attended_gradient.1.refs_1_, bf16[128,2048]{1,0:T(8,128)(2,1)} %collective-permute-done.refs_2_.refs_3_, ...), custom_call_target="tpu_custom_call" | custom-call | flops 402653184 | bytes 8388608 | tf_op jit(solution)/shard_map/head_forward/pallas_call | solution.py:121
  37.2 6.0 %all-to-all-start.1 = ((bf16[16,256,128]{2,1,0:T(8,128)(2,1)}), bf16[16,256,128]{2,1,0:T(8,128)(2,1)S(1)}, u32[]{:S(2)}, u32[]{:S(2)}) async-start(bf16[16,256,128]{2,1,0:T(8,128)(2,1)} %get-tuple-element.20.refs_1_), calls=%async_computation.1 | async-start | bytes 2097152 | tf_op jit(solution)/shard_map/all_to_all | solution.py:634
  43.3 1.6 %collective-permute-start.3 = (bf16[128,2048]{1,0:T(8,128)(2,1)}, bf16[128,2048]{1,0:T(8,128)(2,1)}, u32[]{:S(2)}, u32[]{:S(2)}) collective-permute-start(bf16[128,2048]{1,0:T(8,128)(2,1)} %collective-permute-done.2.refs_4_.refs_8_), channel_id=1, source_target_pairs={{0,32},{16,48},{32,0},{48,16},{64,96},{80,112},{96,64},{112,80},{1... | collective-permute-start | bytes 1572872 | tf_op jit(solution)/shard_map/ppermute | solution.py:639
  44.8 1.8 %collective-permute-start.6 = (bf16[128,2048]{1,0:T(8,128)(2,1)}, bf16[128,2048]{1,0:T(8,128)(2,1)}, u32[]{:S(2)}, u32[]{:S(2)}) collective-permute-start(bf16[128,2048]{1,0:T(8,128)(2,1)} %collective-permute-done.2.refs_4_.refs_8_), channel_id=1, source_target_pairs={{0,16},{16,0},{32,48},{48,32},{64,80},{80,64},{96,112},{112,96},{1... | collective-permute-start | bytes 1572872 | tf_op jit(solution)/shard_map/ppermute | solution.py:639
  46.7 0.0 collective-permute-start.4
  46.7 10.6 %collective-permute-done.3.refs_7_.refs_6_ = bf16[128,2048]{1,0:T(8,128)(2,1)} collective-permute-done((bf16[128,2048]{1,0:T(8,128)(2,1)}, bf16[128,2048]{1,0:T(8,128)(2,1)}, u32[]{:S(2)}, u32[]{:S(2)}) %collective-permute-start.3) | collective-permute-done | bytes 524320 | tf_op jit(solution)/shard_map/ppermute | solution.py:639
  57.3 1.0 collective-permute-start.5
  58.3 2.5 %all-to-all-done.1.refs_0_ = bf16[16,256,128]{2,1,0:T(8,128)(2,1)S(1)} async-done(((bf16[16,256,128]{2,1,0:T(8,128)(2,1)}), bf16[16,256,128]{2,1,0:T(8,128)(2,1)S(1)}, u32[]{:S(2)}, u32[]{:S(2)}) %all-to-all-start.1) | async-done | bytes 1048608 | tf_op jit(solution)/shard_map/all_to_all | solution.py:634
  60.7 1.0 split_attended.1
  61.7 5.2 %all-to-all-start.2 = ((bf16[16,128,128]{2,1,0:T(8,128)(2,1)}), bf16[16,128,128]{2,1,0:T(8,128)(2,1)}, u32[]{:S(2)}, u32[]{:S(2)}) async-start(bf16[16,128,128]{2,1,0:T(8,128)(2,1)} %get-tuple-element.24.refs_5_), calls=%async_computation.2 | async-start | bytes 1048576 | tf_op jit(solution)/shard_map/all_to_all | solution.py:634
  66.9 7.4 %head_backward.1 = (bf16[16,640,128]{2,1,0:T(8,128)(2,1)}, bf16[128,2048]{1,0:T(8,128)(2,1)}) custom-call(bf16[2048,128]{1,0:T(8,128)(2,1)} %bitcast.1, bf16[16,256,128]{2,1,0:T(8,128)(2,1)} %get-tuple-element.20.refs_1_, f32[16,128]{1,0:T(8,128)} %get-tuple-element.22.refs_2_, bf16[3,1792,128]{2,1,0:T(8,128)(2,1)} %get-tuple-element.23.refs_3_, ...), custom_call_target="tpu_custom_call" | custom-call | flops 2080374784 | bytes 25165824 | tf_op jit(solution)/shard_map/head_backward/pallas_call | solution.py:121
  74.3 0.0 collective-permute-done.6.refs_9_
  74.4 0.0 collective-permute-done.4.refs_5_
  74.4 0.0 collective-permute-done.5.refs_7_
  74.4 3.0 %all-to-all-done.2.refs_1_ = bf16[16,128,128]{2,1,0:T(8,128)(2,1)} async-done(((bf16[16,128,128]{2,1,0:T(8,128)(2,1)}), bf16[16,128,128]{2,1,0:T(8,128)(2,1)}, u32[]{:S(2)}, u32[]{:S(2)}) %all-to-all-start.2) | async-done | bytes 524320 | tf_op jit(solution)/shard_map/all_to_all | solution.py:634
  77.4 4.2 %projection_tile.1 = bf16[16,640,128]{2,1,0:T(8,128)(2,1)} custom-call(bf16[16,640,128]{2,1,0:T(8,128)(2,1)} %get-tuple-element.26.refs_0_, bf16[16,128,128]{2,1,0:T(8,128)(2,1)} %all-to-all-done.2.refs_1_, bf16[128,2048]{1,0:T(8,128)(2,1)} %refs_2_.5, bf16[128,2048]{1,0:T(8,128)(2,1)} %collective-permute-done.refs_2_.refs_3_, ...), custom_call_target="tpu_custom_call", output_to_operand_aliasing={{}: (0, {})} | custom-call | flops 1073741824 | bytes 10485760 | tf_op jit(solution)/shard_map/projection_tile/pallas_call | solution.py:121
  81.6 37.8 %all_to_all.20.refs_0_ = bf16[16,640,128]{2,1,0:T(8,128)(2,1)S(1)} all-to-all(bf16[16,640,128]{2,1,0:T(8,128)(2,1)} %projection_tile.1), channel_id=1, replica_groups=mesh['outer'=8,'inner'=16] {'inner'}, dimensions={0} | all-to-all | bytes 5242880 | tf_op jit(solution)/shard_map/all_to_all | solution.py:634
  119.3 1.3 %unpack_grads.1 = (bf16[128,2048]{1,0:T(8,128)(2,1)}, bf16[128,2048]{1,0:T(8,128)(2,1)}, bf16[128,2048]{1,0:T(8,128)(2,1)}, f32[16,2048]{1,0:T(8,128)}) custom-call(bf16[16,640,128]{2,1,0:T(8,128)(2,1)S(1)} %all_to_all.20.refs_0_), custom_call_target="tpu_custom_call" | custom-call | bytes 6291456 | tf_op jit(solution)/shard_map/unpack_grads/pallas_call | solution.py:121
Async XLA Ops:
  3.1 29.0 %all-to-all-start = ((bf16[16,384,128]{2,1,0:T(8,128)(2,1)}), bf16[16,384,128]{2,1,0:T(8,128)(2,1)}, u32[]{:S(2)}, u32[]{:S(2)}) async-start(bf16[16,384,128]{2,1,0:T(8,128)(2,1)} %get-tuple-element.18), calls=%async_computation | async-start | bytes 3145728 | tf_op jit(solution)/shard_map/all_to_all | solution.py:634
  11.3 13.4 %collective-permute-start.2 = (bf16[128,2048]{1,0:T(8,128)(2,1)}, bf16[128,2048]{1,0:T(8,128)(2,1)}, u32[]{:S(2)}, u32[]{:S(2)}) collective-permute-start(bf16[128,2048]{1,0:T(8,128)(2,1)} %refs_2_.5), channel_id=1, source_target_pairs={{0,96},{16,112},{32,64},{48,80},{64,32},{80,48},{96,0},{112,16},{1... | collective-permute-start | bytes 1572872 | tf_op jit(solution)/shard_map/ppermute | solution.py:639
  14.1 11.4 %collective-permute-start.1 = (bf16[128,2048]{1,0:T(8,128)(2,1)}, bf16[128,2048]{1,0:T(8,128)(2,1)}, u32[]{:S(2)}, u32[]{:S(2)}) collective-permute-start(bf16[128,2048]{1,0:T(8,128)(2,1)} %refs_2_.5), channel_id=1, source_target_pairs={{0,32},{16,48},{32,0},{48,16},{64,96},{80,112},{96,64},{112,80},{1... | collective-permute-start | bytes 1572872 | tf_op jit(solution)/shard_map/ppermute | solution.py:639
  14.3 11.2 %collective-permute-start = (bf16[128,2048]{1,0:T(8,128)(2,1)}, bf16[128,2048]{1,0:T(8,128)(2,1)}, u32[]{:S(2)}, u32[]{:S(2)}) collective-permute-start(bf16[128,2048]{1,0:T(8,128)(2,1)} %refs_2_.5), channel_id=1, source_target_pairs={{0,16},{16,0},{32,48},{48,32},{64,80},{80,64},{96,112},{112,96},{1... | collective-permute-start | bytes 1572872 | tf_op jit(solution)/shard_map/ppermute | solution.py:639
  37.2 23.5 %all-to-all-start.1 = ((bf16[16,256,128]{2,1,0:T(8,128)(2,1)}), bf16[16,256,128]{2,1,0:T(8,128)(2,1)S(1)}, u32[]{:S(2)}, u32[]{:S(2)}) async-start(bf16[16,256,128]{2,1,0:T(8,128)(2,1)} %get-tuple-element.20.refs_1_), calls=%async_computation.1 | async-start | bytes 2097152 | tf_op jit(solution)/shard_map/all_to_all | solution.py:634
  43.3 14.0 %collective-permute-start.3 = (bf16[128,2048]{1,0:T(8,128)(2,1)}, bf16[128,2048]{1,0:T(8,128)(2,1)}, u32[]{:S(2)}, u32[]{:S(2)}) collective-permute-start(bf16[128,2048]{1,0:T(8,128)(2,1)} %collective-permute-done.2.refs_4_.refs_8_), channel_id=1, source_target_pairs={{0,32},{16,48},{32,0},{48,16},{64,96},{80,112},{96,64},{112,80},{1... | collective-permute-start | bytes 1572872 | tf_op jit(solution)/shard_map/ppermute | solution.py:639
  44.8 29.5 %collective-permute-start.6 = (bf16[128,2048]{1,0:T(8,128)(2,1)}, bf16[128,2048]{1,0:T(8,128)(2,1)}, u32[]{:S(2)}, u32[]{:S(2)}) collective-permute-start(bf16[128,2048]{1,0:T(8,128)(2,1)} %collective-permute-done.2.refs_4_.refs_8_), channel_id=1, source_target_pairs={{0,16},{16,0},{32,48},{48,32},{64,80},{80,64},{96,112},{112,96},{1... | collective-permute-start | bytes 1572872 | tf_op jit(solution)/shard_map/ppermute | solution.py:639
  46.7 27.7 %collective-permute-start.4 = (bf16[128,2048]{1,0:T(8,128)(2,1)}, bf16[128,2048]{1,0:T(8,128)(2,1)}, u32[]{:S(2)}, u32[]{:S(2)}) collective-permute-start(bf16[128,2048]{1,0:T(8,128)(2,1)} %collective-permute-done.1.refs_3_.refs_4_), channel_id=1, source_target_pairs={{0,16},{16,0},{32,48},{48,32},{64,80},{80,64},{96,112},{112,96},{1... | collective-permute-start | bytes 1572872 | tf_op jit(solution)/shard_map/ppermute | solution.py:639
  57.3 17.1 %collective-permute-start.5 = (bf16[128,2048]{1,0:T(8,128)(2,1)}, bf16[128,2048]{1,0:T(8,128)(2,1)}, u32[]{:S(2)}, u32[]{:S(2)}) collective-permute-start(bf16[128,2048]{1,0:T(8,128)(2,1)} %collective-permute-done.3.refs_7_.refs_6_), channel_id=1, source_target_pairs={{0,16},{16,0},{32,48},{48,32},{64,80},{80,64},{96,112},{112,96},{1... | collective-permute-start | bytes 1572872 | tf_op jit(solution)/shard_map/ppermute | solution.py:639
  61.7 15.6 %all-to-all-start.2 = ((bf16[16,128,128]{2,1,0:T(8,128)(2,1)}), bf16[16,128,128]{2,1,0:T(8,128)(2,1)}, u32[]{:S(2)}, u32[]{:S(2)}) async-start(bf16[16,128,128]{2,1,0:T(8,128)(2,1)} %get-tuple-element.24.refs_5_), calls=%async_computation.2 | async-start | bytes 1048576 | tf_op jit(solution)/shard_map/all_to_all | solution.py:634

commit v3 on v1

--- a/solution.py
+++ b/solution.py
@@ -438,7 +438,7 @@
             ((BLOCK, w_out.shape[1]), BF16, "vmem"),
         ],
         ["hbm"] * 7,
-        63.6,
+        63.4,
         scratch=[
             pltpu.VMEM((blocks, 3 * BLOCK, WIDTH), BF16),
             pltpu.VMEM(rows.shape, BF16),
@@ -460,13 +460,11 @@
     )(grad.reshape(tokens, WIDTH), sent, lse, lev, qkv, rows, w_out)
 
 
-def tile_body(groups, per, _, att_in, *refs):
+def tile_body(groups, per, _, att_ref, *refs):
     cot_refs = refs[:groups]
-    out_ref, att_ref, lhs, held, tile, sems = refs[groups:]
+    out_ref, lhs, held, tile, sems = refs[groups:]
     chunk = lhs.shape[0] // HEADS
     chunks, step = held.shape[0], held.shape[2]
-    att_copy = pltpu.make_async_copy(att_in, att_ref, sems.at[0])
-    att_copy.start()
     copies, stores = [], []
     for c in range(chunks):
         for k, ref in enumerate(cot_refs):
@@ -478,7 +476,6 @@
                 )
             )
             copies[-1].start()
-    att_copy.wait()
     mine = lax.axis_index("outer")
     for k in range(groups):
         for j in range(per):
@@ -517,10 +514,9 @@
     return kernel_call(
         functools.partial(tile_body, groups, per),
         [(grads.shape, BF16, "hbm")],
-        ["hbm"] * (2 + groups),
+        ["hbm", "vmem"] + ["hbm"] * groups,
         18,
         scratch=[
-            pltpu.VMEM(att.shape, BF16),
             pltpu.VMEM((per * WIDTH, groups * BLOCK), BF16),
             pltpu.VMEM((chunks, groups * BLOCK, width // chunks), BF16),
             pltpu.VMEM((HEADS, extra, WIDTH), BF16),

time: 121 us -> 121 us (level)
  no operation moved by 1% of the time
where the time goes in v3:
time: 121 us; the launch traced here: 120 us
  blocking collectives  37.8 us (31%)
  waiting for transfers between devices  32.2 us (27%)
  Pallas kernels  28.3 us (23%)
  starting transfers between devices  21.3 us (18%)
    all_to_all x1, blocking collectives, swap(): return lax.all_to_all(value, axis, 0, 0, tiled=True)  37.8 us
    pallas_call x7, Pallas kernels, run(): return call(*operands)  28.3 us
    ppermute x7, waiting for transfers between devices, from_outer(): return lax.ppermute(value, 'outer', [(i, i ^ apart) for i in range(size)])  17.4 us
    all_to_all x3, starting transfers between devices, swap(): return lax.all_to_all(value, axis, 0, 0, tiled=True)  16.2 us
    all_to_all x3, waiting for transfers between devices, swap(): return lax.all_to_all(value, axis, 0, 0, tiled=True)  14.8 us
    ppermute x7, starting transfers between devices, from_outer(): return lax.ppermute(value, 'outer', [(i, i ^ apart) for i in range(size)])  5.15 us
  transfers between devices with their start and end apart: 10, of which 6 were waited for; matrix products, arithmetic and copies ran while one was open for 0% of the time, Pallas kernels for 13%

profile of v3, /device:TPU:0, one launch (start us, length us, event | category | flops | bytes accessed | tf_op | source)
XLA Modules:
  0.0 120.4 jit_solution(5710711709951889711)
XLA Ops:
  0.6 2.4 %pack_qkv.1 = bf16[16,384,128]{2,1,0:T(8,128)(2,1)} custom-call(bf16[128,2048]{1,0:T(8,128)(2,1)} %refs_0_.2, bf16[128,2048]{1,0:T(8,128)(2,1)} %refs_1_.2, bf16[128,2048]{1,0:T(8,128)(2,1)} %refs_2_.2), custom_call_target="tpu_custom_call" | custom-call | bytes 3145728 | tf_op jit(solution)/shard_map/pack_qkv/pallas_call | solution.py:120
  3.0 8.2 %all-to-all-start = ((bf16[16,384,128]{2,1,0:T(8,128)(2,1)}), bf16[16,384,128]{2,1,0:T(8,128)(2,1)}, u32[]{:S(2)}, u32[]{:S(2)}) async-start(bf16[16,384,128]{2,1,0:T(8,128)(2,1)} %pack_qkv.1), calls=%async_computation | async-start | bytes 3145728 | tf_op jit(solution)/shard_map/all_to_all | solution.py:596
  11.2 2.8 %collective-permute-start.2 = (bf16[128,2048]{1,0:T(8,128)(2,1)}, bf16[128,2048]{1,0:T(8,128)(2,1)}, u32[]{:S(2)}, u32[]{:S(2)}) collective-permute-start(bf16[128,2048]{1,0:T(8,128)(2,1)} %refs_2_.3), channel_id=1, source_target_pairs={{0,96},{16,112},{32,64},{48,80},{64,32},{80,48},{96,0},{112,16},{1... | collective-permute-start | bytes 1572872 | tf_op jit(solution)/shard_map/ppermute | solution.py:601
  14.0 0.2 collective-permute-start.1
  14.3 0.0 collective-permute-start
  14.3 6.8 %attended_gradient.1.refs_1_ = bf16[128,2048]{1,0:T(8,128)(2,1)} custom-call(bf16[128,2048]{1,0:T(8,128)(2,1)} %refs_2_.3, bf16[2048,2048]{1,0:T(8,128)(2,1)} %refs_6_.1), custom_call_target="tpu_custom_call" | custom-call | bytes 1048576 | tf_op jit(solution)/shard_map/attended_gradient/pallas_call | solution.py:120
  21.1 5.1 %collective-permute-done.2.refs_4_.refs_8_ = bf16[128,2048]{1,0:T(8,128)(2,1)} collective-permute-done((bf16[128,2048]{1,0:T(8,128)(2,1)}, bf16[128,2048]{1,0:T(8,128)(2,1)}, u32[]{:S(2)}, u32[]{:S(2)}) %collective-permute-start.2) | collective-permute-done | bytes 524320 | tf_op jit(solution)/shard_map/ppermute | solution.py:601
  26.2 1.3 %collective-permute-done.1.refs_3_.refs_4_ = bf16[128,2048]{1,0:T(8,128)(2,1)} collective-permute-done((bf16[128,2048]{1,0:T(8,128)(2,1)}, bf16[128,2048]{1,0:T(8,128)(2,1)}, u32[]{:S(2)}, u32[]{:S(2)}) %collective-permute-start.1) | collective-permute-done | bytes 524320 | tf_op jit(solution)/shard_map/ppermute | solution.py:601
  27.5 0.0 collective-permute-done.refs_2_.refs_3_
  27.5 8.3 %all-to-all-done.refs_0_.refs_4_ = bf16[16,384,128]{2,1,0:T(8,128)(2,1)} async-done(((bf16[16,384,128]{2,1,0:T(8,128)(2,1)}), bf16[16,384,128]{2,1,0:T(8,128)(2,1)}, u32[]{:S(2)}, u32[]{:S(2)}) %all-to-all-start) | async-done | bytes 1572896 | tf_op jit(solution)/shard_map/all_to_all | solution.py:596
  35.7 5.2 %head_forward.1 = (bf16[16,256,128]{2,1,0:T(8,128)(2,1)}, f32[16,128]{1,0:T(8,128)}, bf16[3,1792,128]{2,1,0:T(8,128)(2,1)}) custom-call(bf16[16,384,128]{2,1,0:T(8,128)(2,1)} %all-to-all-done.refs_0_.refs_4_, bf16[128,2048]{1,0:T(8,128)(2,1)} %attended_gradient.1.refs_1_, bf16[128,2048]{1,0:T(8,128)(2,1)} %collective-permute-done.refs_2_.refs_3_, ...), custom_call_target="tpu_custom_call" | custom-call | flops 402653184 | bytes 8388608 | tf_op jit(solution)/shard_map/head_forward/pallas_call | solution.py:120
  40.9 3.7 %all-to-all-start.1 = ((bf16[16,256,128]{2,1,0:T(8,128)(2,1)}), bf16[16,256,128]{2,1,0:T(8,128)(2,1)S(1)}, u32[]{:S(2)}, u32[]{:S(2)}) async-start(bf16[16,256,128]{2,1,0:T(8,128)(2,1)} %get-tuple-element.16.refs_1_), calls=%async_computation.1 | async-start | bytes 2097152 | tf_op jit(solution)/shard_map/all_to_all | solution.py:596
  44.6 1.6 %collective-permute-start.3 = (bf16[128,2048]{1,0:T(8,128)(2,1)}, bf16[128,2048]{1,0:T(8,128)(2,1)}, u32[]{:S(2)}, u32[]{:S(2)}) collective-permute-start(bf16[128,2048]{1,0:T(8,128)(2,1)} %collective-permute-done.2.refs_4_.refs_8_), channel_id=1, source_target_pairs={{0,32},{16,48},{32,0},{48,16},{64,96},{80,112},{96,64},{112,80},{1... | collective-permute-start | bytes 1572872 | tf_op jit(solution)/shard_map/ppermute | solution.py:601
  46.1 0.0 collective-permute-start.6
  46.1 0.5 collective-permute-start.4
  46.7 11.0 %collective-permute-done.3.refs_7_.refs_6_ = bf16[128,2048]{1,0:T(8,128)(2,1)} collective-permute-done((bf16[128,2048]{1,0:T(8,128)(2,1)}, bf16[128,2048]{1,0:T(8,128)(2,1)}, u32[]{:S(2)}, u32[]{:S(2)}) %collective-permute-start.3) | collective-permute-done | bytes 524320 | tf_op jit(solution)/shard_map/ppermute | solution.py:601
  57.7 0.0 collective-permute-start.5
  57.7 3.7 %all-to-all-done.1.refs_0_ = bf16[16,256,128]{2,1,0:T(8,128)(2,1)S(1)} async-done(((bf16[16,256,128]{2,1,0:T(8,128)(2,1)}), bf16[16,256,128]{2,1,0:T(8,128)(2,1)S(1)}, u32[]{:S(2)}, u32[]{:S(2)}) %all-to-all-start.1) | async-done | bytes 1048608 | tf_op jit(solution)/shard_map/all_to_all | solution.py:596
  61.3 1.0 split_attended.1
  62.3 4.3 %all-to-all-start.2 = ((bf16[16,128,128]{2,1,0:T(8,128)(2,1)}), bf16[16,128,128]{2,1,0:T(8,128)(2,1)S(1)}, u32[]{:S(2)}, u32[]{:S(2)}) async-start(bf16[16,128,128]{2,1,0:T(8,128)(2,1)} %get-tuple-element.20.refs_5_), calls=%async_computation.2 | async-start | bytes 1048576 | tf_op jit(solution)/shard_map/all_to_all | solution.py:596
  66.6 7.4 %head_backward.1 = (bf16[16,640,128]{2,1,0:T(8,128)(2,1)}, bf16[128,2048]{1,0:T(8,128)(2,1)}) custom-call(bf16[2048,128]{1,0:T(8,128)(2,1)} %bitcast.1, bf16[16,256,128]{2,1,0:T(8,128)(2,1)} %get-tuple-element.16.refs_1_, f32[16,128]{1,0:T(8,128)} %get-tuple-element.18.refs_2_, bf16[3,1792,128]{2,1,0:T(8,128)(2,1)} %get-tuple-element.19.refs_3_, ...), custom_call_target="tpu_custom_call" | custom-call | flops 2080374784 | bytes 25165824 | tf_op jit(solution)/shard_map/head_backward/pallas_call | solution.py:120
  74.1 0.0 collective-permute-done.6.refs_9_
  74.1 0.0 collective-permute-done.4.refs_5_
  74.1 0.0 collective-permute-done.5.refs_7_
  74.1 2.9 %all-to-all-done.2.refs_1_ = bf16[16,128,128]{2,1,0:T(8,128)(2,1)S(1)} async-done(((bf16[16,128,128]{2,1,0:T(8,128)(2,1)}), bf16[16,128,128]{2,1,0:T(8,128)(2,1)S(1)}, u32[]{:S(2)}, u32[]{:S(2)}) %all-to-all-start.2) | async-done | bytes 524320 | tf_op jit(solution)/shard_map/all_to_all | solution.py:596
  77.0 4.2 %projection_tile.1 = bf16[16,640,128]{2,1,0:T(8,128)(2,1)} custom-call(bf16[16,640,128]{2,1,0:T(8,128)(2,1)} %get-tuple-element.22.refs_0_, bf16[16,128,128]{2,1,0:T(8,128)(2,1)S(1)} %all-to-all-done.2.refs_1_, bf16[128,2048]{1,0:T(8,128)(2,1)} %refs_2_.3, bf16[128,2048]{1,0:T(8,128)(2,1)} %collective-permute-done.refs_2_.refs_3_, ...), custom_call_target="tpu_custom_call", output_to_operand_aliasing={{}: (0, {})} | custom-call | flops 1073741824 | bytes 10485760 | tf_op jit(solution)/shard_map/projection_tile/pallas_call | solution.py:120
  81.1 37.8 %all_to_all.20.refs_0_ = bf16[16,640,128]{2,1,0:T(8,128)(2,1)S(1)} all-to-all(bf16[16,640,128]{2,1,0:T(8,128)(2,1)} %projection_tile.1), channel_id=1, replica_groups=mesh['outer'=8,'inner'=16] {'inner'}, dimensions={0} | all-to-all | bytes 5242880 | tf_op jit(solution)/shard_map/all_to_all | solution.py:596
  118.9 1.3 %unpack_grads.1 = (bf16[128,2048]{1,0:T(8,128)(2,1)}, bf16[128,2048]{1,0:T(8,128)(2,1)}, bf16[128,2048]{1,0:T(8,128)(2,1)}, f32[16,2048]{1,0:T(8,128)}) custom-call(bf16[16,640,128]{2,1,0:T(8,128)(2,1)S(1)} %all_to_all.20.refs_0_), custom_call_target="tpu_custom_call" | custom-call | bytes 6291456 | tf_op jit(solution)/shard_map/unpack_grads/pallas_call | solution.py:120
Async XLA Ops:
  3.0 32.7 %all-to-all-start = ((bf16[16,384,128]{2,1,0:T(8,128)(2,1)}), bf16[16,384,128]{2,1,0:T(8,128)(2,1)}, u32[]{:S(2)}, u32[]{:S(2)}) async-start(bf16[16,384,128]{2,1,0:T(8,128)(2,1)} %pack_qkv.1), calls=%async_computation | async-start | bytes 3145728 | tf_op jit(solution)/shard_map/all_to_all | solution.py:596
  11.2 15.0 %collective-permute-start.2 = (bf16[128,2048]{1,0:T(8,128)(2,1)}, bf16[128,2048]{1,0:T(8,128)(2,1)}, u32[]{:S(2)}, u32[]{:S(2)}) collective-permute-start(bf16[128,2048]{1,0:T(8,128)(2,1)} %refs_2_.3), channel_id=1, source_target_pairs={{0,96},{16,112},{32,64},{48,80},{64,32},{80,48},{96,0},{112,16},{1... | collective-permute-start | bytes 1572872 | tf_op jit(solution)/shard_map/ppermute | solution.py:601
  14.0 13.4 %collective-permute-start.1 = (bf16[128,2048]{1,0:T(8,128)(2,1)}, bf16[128,2048]{1,0:T(8,128)(2,1)}, u32[]{:S(2)}, u32[]{:S(2)}) collective-permute-start(bf16[128,2048]{1,0:T(8,128)(2,1)} %refs_2_.3), channel_id=1, source_target_pairs={{0,32},{16,48},{32,0},{48,16},{64,96},{80,112},{96,64},{112,80},{1... | collective-permute-start | bytes 1572872 | tf_op jit(solution)/shard_map/ppermute | solution.py:601
  14.3 13.2 %collective-permute-start = (bf16[128,2048]{1,0:T(8,128)(2,1)}, bf16[128,2048]{1,0:T(8,128)(2,1)}, u32[]{:S(2)}, u32[]{:S(2)}) collective-permute-start(bf16[128,2048]{1,0:T(8,128)(2,1)} %refs_2_.3), channel_id=1, source_target_pairs={{0,16},{16,0},{32,48},{48,32},{64,80},{80,64},{96,112},{112,96},{1... | collective-permute-start | bytes 1572872 | tf_op jit(solution)/shard_map/ppermute | solution.py:601
  40.9 20.4 %all-to-all-start.1 = ((bf16[16,256,128]{2,1,0:T(8,128)(2,1)}), bf16[16,256,128]{2,1,0:T(8,128)(2,1)S(1)}, u32[]{:S(2)}, u32[]{:S(2)}) async-start(bf16[16,256,128]{2,1,0:T(8,128)(2,1)} %get-tuple-element.16.refs_1_), calls=%async_computation.1 | async-start | bytes 2097152 | tf_op jit(solution)/shard_map/all_to_all | solution.py:596
  44.6 13.1 %collective-permute-start.3 = (bf16[128,2048]{1,0:T(8,128)(2,1)}, bf16[128,2048]{1,0:T(8,128)(2,1)}, u32[]{:S(2)}, u32[]{:S(2)}) collective-permute-start(bf16[128,2048]{1,0:T(8,128)(2,1)} %collective-permute-done.2.refs_4_.refs_8_), channel_id=1, source_target_pairs={{0,32},{16,48},{32,0},{48,16},{64,96},{80,112},{96,64},{112,80},{1... | collective-permute-start | bytes 1572872 | tf_op jit(solution)/shard_map/ppermute | solution.py:601
  46.1 27.9 %collective-permute-start.6 = (bf16[128,2048]{1,0:T(8,128)(2,1)}, bf16[128,2048]{1,0:T(8,128)(2,1)}, u32[]{:S(2)}, u32[]{:S(2)}) collective-permute-start(bf16[128,2048]{1,0:T(8,128)(2,1)} %collective-permute-done.2.refs_4_.refs_8_), channel_id=1, source_target_pairs={{0,16},{16,0},{32,48},{48,32},{64,80},{80,64},{96,112},{112,96},{1... | collective-permute-start | bytes 1572872 | tf_op jit(solution)/shard_map/ppermute | solution.py:601
  46.1 28.0 %collective-permute-start.4 = (bf16[128,2048]{1,0:T(8,128)(2,1)}, bf16[128,2048]{1,0:T(8,128)(2,1)}, u32[]{:S(2)}, u32[]{:S(2)}) collective-permute-start(bf16[128,2048]{1,0:T(8,128)(2,1)} %collective-permute-done.1.refs_3_.refs_4_), channel_id=1, source_target_pairs={{0,16},{16,0},{32,48},{48,32},{64,80},{80,64},{96,112},{112,96},{1... | collective-permute-start | bytes 1572872 | tf_op jit(solution)/shard_map/ppermute | solution.py:601
  57.7 16.4 %collective-permute-start.5 = (bf16[128,2048]{1,0:T(8,128)(2,1)}, bf16[128,2048]{1,0:T(8,128)(2,1)}, u32[]{:S(2)}, u32[]{:S(2)}) collective-permute-start(bf16[128,2048]{1,0:T(8,128)(2,1)} %collective-permute-done.3.refs_7_.refs_6_), channel_id=1, source_target_pairs={{0,16},{16,0},{32,48},{48,32},{64,80},{80,64},{96,112},{112,96},{1... | collective-permute-start | bytes 1572872 | tf_op jit(solution)/shard_map/ppermute | solution.py:601
  62.3 14.7 %all-to-all-start.2 = ((bf16[16,128,128]{2,1,0:T(8,128)(2,1)}), bf16[16,128,128]{2,1,0:T(8,128)(2,1)S(1)}, u32[]{:S(2)}, u32[]{:S(2)}) async-start(bf16[16,128,128]{2,1,0:T(8,128)(2,1)} %get-tuple-element.20.refs_5_), calls=%async_computation.2 | async-start | bytes 1048576 | tf_op jit(solution)/shard_map/all_to_all | solution.py:596

commit v4 on v1

--- a/solution.py
+++ b/solution.py
@@ -131,20 +131,23 @@
 
 
 def pack_body(q_ref, k_ref, v_ref, out_ref, held, packed, in_sems, out_sems):
-    loads = [
-        pltpu.make_async_copy(ref, held.at[x], in_sems.at[x])
-        for x, ref in enumerate((q_ref, k_ref, v_ref))
-    ]
-    for load in loads:
-        load.start()
-    stores = []
-    for x, load in enumerate(loads):
-        load.wait()
-        rows = slice(x * BLOCK, (x + 1) * BLOCK)
+    half = BLOCK // 2
+    jobs = [(x, first) for x in range(3) for first in (0, half)]
+    loads, stores = [], []
+    for i, (x, first) in enumerate(jobs):
+        rows = slice(first, first + half)
+        ref = (q_ref, k_ref, v_ref)[x]
+        loads.append(
+            pltpu.make_async_copy(ref.at[rows, :], held.at[x, rows, :], in_sems.at[i])
+        )
+        loads[-1].start()
+    for i, (x, first) in enumerate(jobs):
+        loads[i].wait()
+        rows = slice(x * BLOCK + first, x * BLOCK + first + half)
         for h in range(HEADS):
-            packed[h, rows, :] = held[x, :, h * WIDTH : (h + 1) * WIDTH]
+            packed[h, rows, :] = held[x, first : first + half, h * WIDTH : (h + 1) * WIDTH]
         stores.append(
-            pltpu.make_async_copy(packed.at[:, rows, :], out_ref.at[:, rows, :], out_sems.at[x])
+            pltpu.make_async_copy(packed.at[:, rows, :], out_ref.at[:, rows, :], out_sems.at[i])
         )
         stores[-1].start()
     for store in stores:
@@ -158,7 +161,7 @@
         [(packed, BF16, "hbm")],
         ["hbm"] * 3,
         6,
-        scratch=[pltpu.VMEM((3,) + q.shape, BF16), pltpu.VMEM(packed, BF16), dma(3), dma(3)],
+        scratch=[pltpu.VMEM((3,) + q.shape, BF16), pltpu.VMEM(packed, BF16), dma(6), dma(6)],
         cost=cost(0, 6 * q.size * 2),
         name="pack_qkv",
     )(q, k, v)[0]

time: 121 us -> 121 us (level)
  no operation moved by 1% of the time
where the time goes in v4:
time: 121 us; the launch traced here: 120 us
  blocking collectives  37.8 us (31%)
  waiting for transfers between devices  32.2 us (27%)
  Pallas kernels  28.2 us (23%)
  starting transfers between devices  21.3 us (18%)
    all_to_all x1, blocking collectives, swap(): return lax.all_to_all(value, axis, 0, 0, tiled=True)  37.8 us
    pallas_call x7, Pallas kernels, run(): return call(*operands)  28.2 us
    ppermute x7, waiting for transfers between devices, from_outer(): return lax.ppermute(value, 'outer', [(i, i ^ apart) for i in range(size)])  17.4 us
    all_to_all x3, starting transfers between devices, swap(): return lax.all_to_all(value, axis, 0, 0, tiled=True)  16.2 us
    all_to_all x3, waiting for transfers between devices, swap(): return lax.all_to_all(value, axis, 0, 0, tiled=True)  14.8 us
    ppermute x7, starting transfers between devices, from_outer(): return lax.ppermute(value, 'outer', [(i, i ^ apart) for i in range(size)])  5.15 us
  transfers between devices with their start and end apart: 10, of which 6 were waited for; matrix products, arithmetic and copies ran while one was open for 0% of the time, Pallas kernels for 13%

profile of v4, /device:TPU:0, one launch (start us, length us, event | category | flops | bytes accessed | tf_op | source)
XLA Modules:
  0.0 120.4 jit_solution(5841897453204352640)
XLA Ops:
  0.6 2.3 %pack_qkv.1 = bf16[16,384,128]{2,1,0:T(8,128)(2,1)} custom-call(bf16[128,2048]{1,0:T(8,128)(2,1)} %refs_0_.2, bf16[128,2048]{1,0:T(8,128)(2,1)} %refs_1_.2, bf16[128,2048]{1,0:T(8,128)(2,1)} %refs_2_.2), custom_call_target="tpu_custom_call" | custom-call | bytes 3145728 | tf_op jit(solution)/shard_map/pack_qkv/pallas_call | solution.py:120
  2.9 8.2 %all-to-all-start = ((bf16[16,384,128]{2,1,0:T(8,128)(2,1)}), bf16[16,384,128]{2,1,0:T(8,128)(2,1)}, u32[]{:S(2)}, u32[]{:S(2)}) async-start(bf16[16,384,128]{2,1,0:T(8,128)(2,1)} %pack_qkv.1), calls=%async_computation | async-start | bytes 3145728 | tf_op jit(solution)/shard_map/all_to_all | solution.py:603
  11.1 2.8 %collective-permute-start.2 = (bf16[128,2048]{1,0:T(8,128)(2,1)}, bf16[128,2048]{1,0:T(8,128)(2,1)}, u32[]{:S(2)}, u32[]{:S(2)}) collective-permute-start(bf16[128,2048]{1,0:T(8,128)(2,1)} %refs_2_.3), channel_id=1, source_target_pairs={{0,96},{16,112},{32,64},{48,80},{64,32},{80,48},{96,0},{112,16},{1... | collective-permute-start | bytes 1572872 | tf_op jit(solution)/shard_map/ppermute | solution.py:608
  13.9 0.2 collective-permute-start.1
  14.2 0.0 collective-permute-start
  14.2 6.8 %attended_gradient.1.refs_1_ = bf16[128,2048]{1,0:T(8,128)(2,1)} custom-call(bf16[128,2048]{1,0:T(8,128)(2,1)} %refs_2_.3, bf16[2048,2048]{1,0:T(8,128)(2,1)} %refs_6_.1), custom_call_target="tpu_custom_call" | custom-call | bytes 1048576 | tf_op jit(solution)/shard_map/attended_gradient/pallas_call | solution.py:120
  21.0 5.1 %collective-permute-done.2.refs_4_.refs_8_ = bf16[128,2048]{1,0:T(8,128)(2,1)} collective-permute-done((bf16[128,2048]{1,0:T(8,128)(2,1)}, bf16[128,2048]{1,0:T(8,128)(2,1)}, u32[]{:S(2)}, u32[]{:S(2)}) %collective-permute-start.2) | collective-permute-done | bytes 524320 | tf_op jit(solution)/shard_map/ppermute | solution.py:608
  26.1 1.3 %collective-permute-done.1.refs_3_.refs_4_ = bf16[128,2048]{1,0:T(8,128)(2,1)} collective-permute-done((bf16[128,2048]{1,0:T(8,128)(2,1)}, bf16[128,2048]{1,0:T(8,128)(2,1)}, u32[]{:S(2)}, u32[]{:S(2)}) %collective-permute-start.1) | collective-permute-done | bytes 524320 | tf_op jit(solution)/shard_map/ppermute | solution.py:608
  27.3 0.0 collective-permute-done.refs_2_.refs_3_
  27.3 8.3 %all-to-all-done.refs_0_.refs_4_ = bf16[16,384,128]{2,1,0:T(8,128)(2,1)} async-done(((bf16[16,384,128]{2,1,0:T(8,128)(2,1)}), bf16[16,384,128]{2,1,0:T(8,128)(2,1)}, u32[]{:S(2)}, u32[]{:S(2)}) %all-to-all-start) | async-done | bytes 1572896 | tf_op jit(solution)/shard_map/all_to_all | solution.py:603
  35.6 5.2 %head_forward.1 = (bf16[16,256,128]{2,1,0:T(8,128)(2,1)}, f32[16,128]{1,0:T(8,128)}, bf16[3,1792,128]{2,1,0:T(8,128)(2,1)}) custom-call(bf16[16,384,128]{2,1,0:T(8,128)(2,1)} %all-to-all-done.refs_0_.refs_4_, bf16[128,2048]{1,0:T(8,128)(2,1)} %attended_gradient.1.refs_1_, bf16[128,2048]{1,0:T(8,128)(2,1)} %collective-permute-done.refs_2_.refs_3_, ...), custom_call_target="tpu_custom_call" | custom-call | flops 402653184 | bytes 8388608 | tf_op jit(solution)/shard_map/head_forward/pallas_call | solution.py:120
  40.8 3.7 %all-to-all-start.1 = ((bf16[16,256,128]{2,1,0:T(8,128)(2,1)}), bf16[16,256,128]{2,1,0:T(8,128)(2,1)S(1)}, u32[]{:S(2)}, u32[]{:S(2)}) async-start(bf16[16,256,128]{2,1,0:T(8,128)(2,1)} %get-tuple-element.16.refs_1_), calls=%async_computation.1 | async-start | bytes 2097152 | tf_op jit(solution)/shard_map/all_to_all | solution.py:603
  44.5 1.6 %collective-permute-start.3 = (bf16[128,2048]{1,0:T(8,128)(2,1)}, bf16[128,2048]{1,0:T(8,128)(2,1)}, u32[]{:S(2)}, u32[]{:S(2)}) collective-permute-start(bf16[128,2048]{1,0:T(8,128)(2,1)} %collective-permute-done.2.refs_4_.refs_8_), channel_id=1, source_target_pairs={{0,32},{16,48},{32,0},{48,16},{64,96},{80,112},{96,64},{112,80},{1... | collective-permute-start | bytes 1572872 | tf_op jit(solution)/shard_map/ppermute | solution.py:608
  46.0 0.0 collective-permute-start.6
  46.0 0.5 collective-permute-start.4
  46.5 11.0 %collective-permute-done.3.refs_7_.refs_6_ = bf16[128,2048]{1,0:T(8,128)(2,1)} collective-permute-done((bf16[128,2048]{1,0:T(8,128)(2,1)}, bf16[128,2048]{1,0:T(8,128)(2,1)}, u32[]{:S(2)}, u32[]{:S(2)}) %collective-permute-start.3) | collective-permute-done | bytes 524320 | tf_op jit(solution)/shard_map/ppermute | solution.py:608
  57.6 0.0 collective-permute-start.5
  57.6 3.6 %all-to-all-done.1.refs_0_ = bf16[16,256,128]{2,1,0:T(8,128)(2,1)S(1)} async-done(((bf16[16,256,128]{2,1,0:T(8,128)(2,1)}), bf16[16,256,128]{2,1,0:T(8,128)(2,1)S(1)}, u32[]{:S(2)}, u32[]{:S(2)}) %all-to-all-start.1) | async-done | bytes 1048608 | tf_op jit(solution)/shard_map/all_to_all | solution.py:603
  61.2 1.0 split_attended.1
  62.2 4.3 %all-to-all-start.2 = ((bf16[16,128,128]{2,1,0:T(8,128)(2,1)}), bf16[16,128,128]{2,1,0:T(8,128)(2,1)}, u32[]{:S(2)}, u32[]{:S(2)}) async-start(bf16[16,128,128]{2,1,0:T(8,128)(2,1)} %get-tuple-element.20.refs_5_), calls=%async_computation.2 | async-start | bytes 1048576 | tf_op jit(solution)/shard_map/all_to_all | solution.py:603
  66.6 7.5 %head_backward.1 = (bf16[16,640,128]{2,1,0:T(8,128)(2,1)}, bf16[128,2048]{1,0:T(8,128)(2,1)}) custom-call(bf16[2048,128]{1,0:T(8,128)(2,1)} %bitcast.1, bf16[16,256,128]{2,1,0:T(8,128)(2,1)} %get-tuple-element.16.refs_1_, f32[16,128]{1,0:T(8,128)} %get-tuple-element.18.refs_2_, bf16[3,1792,128]{2,1,0:T(8,128)(2,1)} %get-tuple-element.19.refs_3_, ...), custom_call_target="tpu_custom_call" | custom-call | flops 2080374784 | bytes 25165824 | tf_op jit(solution)/shard_map/head_backward/pallas_call | solution.py:120
  74.0 0.0 collective-permute-done.6.refs_9_
  74.0 0.0 collective-permute-done.4.refs_5_
  74.0 0.0 collective-permute-done.5.refs_7_
  74.1 2.9 %all-to-all-done.2.refs_1_ = bf16[16,128,128]{2,1,0:T(8,128)(2,1)} async-done(((bf16[16,128,128]{2,1,0:T(8,128)(2,1)}), bf16[16,128,128]{2,1,0:T(8,128)(2,1)}, u32[]{:S(2)}, u32[]{:S(2)}) %all-to-all-start.2) | async-done | bytes 524320 | tf_op jit(solution)/shard_map/all_to_all | solution.py:603
  77.0 4.2 %projection_tile.1 = bf16[16,640,128]{2,1,0:T(8,128)(2,1)} custom-call(bf16[16,640,128]{2,1,0:T(8,128)(2,1)} %get-tuple-element.22.refs_0_, bf16[16,128,128]{2,1,0:T(8,128)(2,1)} %all-to-all-done.2.refs_1_, bf16[128,2048]{1,0:T(8,128)(2,1)} %refs_2_.3, bf16[128,2048]{1,0:T(8,128)(2,1)} %collective-permute-done.refs_2_.refs_3_, ...), custom_call_target="tpu_custom_call", output_to_operand_aliasing={{}: (0, {})} | custom-call | flops 1073741824 | bytes 10485760 | tf_op jit(solution)/shard_map/projection_tile/pallas_call | solution.py:120
  81.2 37.8 %all_to_all.20.refs_0_ = bf16[16,640,128]{2,1,0:T(8,128)(2,1)S(1)} all-to-all(bf16[16,640,128]{2,1,0:T(8,128)(2,1)} %projection_tile.1), channel_id=1, replica_groups=mesh['outer'=8,'inner'=16] {'inner'}, dimensions={0} | all-to-all | bytes 5242880 | tf_op jit(solution)/shard_map/all_to_all | solution.py:603
  118.9 1.3 %unpack_grads.1 = (bf16[128,2048]{1,0:T(8,128)(2,1)}, bf16[128,2048]{1,0:T(8,128)(2,1)}, bf16[128,2048]{1,0:T(8,128)(2,1)}, f32[16,2048]{1,0:T(8,128)}) custom-call(bf16[16,640,128]{2,1,0:T(8,128)(2,1)S(1)} %all_to_all.20.refs_0_), custom_call_target="tpu_custom_call" | custom-call | bytes 6291456 | tf_op jit(solution)/shard_map/unpack_grads/pallas_call | solution.py:120
Async XLA Ops:
  2.9 32.7 %all-to-all-start = ((bf16[16,384,128]{2,1,0:T(8,128)(2,1)}), bf16[16,384,128]{2,1,0:T(8,128)(2,1)}, u32[]{:S(2)}, u32[]{:S(2)}) async-start(bf16[16,384,128]{2,1,0:T(8,128)(2,1)} %pack_qkv.1), calls=%async_computation | async-start | bytes 3145728 | tf_op jit(solution)/shard_map/all_to_all | solution.py:603
  11.1 15.0 %collective-permute-start.2 = (bf16[128,2048]{1,0:T(8,128)(2,1)}, bf16[128,2048]{1,0:T(8,128)(2,1)}, u32[]{:S(2)}, u32[]{:S(2)}) collective-permute-start(bf16[128,2048]{1,0:T(8,128)(2,1)} %refs_2_.3), channel_id=1, source_target_pairs={{0,96},{16,112},{32,64},{48,80},{64,32},{80,48},{96,0},{112,16},{1... | collective-permute-start | bytes 1572872 | tf_op jit(solution)/shard_map/ppermute | solution.py:608
  13.9 13.4 %collective-permute-start.1 = (bf16[128,2048]{1,0:T(8,128)(2,1)}, bf16[128,2048]{1,0:T(8,128)(2,1)}, u32[]{:S(2)}, u32[]{:S(2)}) collective-permute-start(bf16[128,2048]{1,0:T(8,128)(2,1)} %refs_2_.3), channel_id=1, source_target_pairs={{0,32},{16,48},{32,0},{48,16},{64,96},{80,112},{96,64},{112,80},{1... | collective-permute-start | bytes 1572872 | tf_op jit(solution)/shard_map/ppermute | solution.py:608
  14.2 13.2 %collective-permute-start = (bf16[128,2048]{1,0:T(8,128)(2,1)}, bf16[128,2048]{1,0:T(8,128)(2,1)}, u32[]{:S(2)}, u32[]{:S(2)}) collective-permute-start(bf16[128,2048]{1,0:T(8,128)(2,1)} %refs_2_.3), channel_id=1, source_target_pairs={{0,16},{16,0},{32,48},{48,32},{64,80},{80,64},{96,112},{112,96},{1... | collective-permute-start | bytes 1572872 | tf_op jit(solution)/shard_map/ppermute | solution.py:608
  40.8 20.4 %all-to-all-start.1 = ((bf16[16,256,128]{2,1,0:T(8,128)(2,1)}), bf16[16,256,128]{2,1,0:T(8,128)(2,1)S(1)}, u32[]{:S(2)}, u32[]{:S(2)}) async-start(bf16[16,256,128]{2,1,0:T(8,128)(2,1)} %get-tuple-element.16.refs_1_), calls=%async_computation.1 | async-start | bytes 2097152 | tf_op jit(solution)/shard_map/all_to_all | solution.py:603
  44.5 13.1 %collective-permute-start.3 = (bf16[128,2048]{1,0:T(8,128)(2,1)}, bf16[128,2048]{1,0:T(8,128)(2,1)}, u32[]{:S(2)}, u32[]{:S(2)}) collective-permute-start(bf16[128,2048]{1,0:T(8,128)(2,1)} %collective-permute-done.2.refs_4_.refs_8_), channel_id=1, source_target_pairs={{0,32},{16,48},{32,0},{48,16},{64,96},{80,112},{96,64},{112,80},{1... | collective-permute-start | bytes 1572872 | tf_op jit(solution)/shard_map/ppermute | solution.py:608
  46.0 28.0 %collective-permute-start.6 = (bf16[128,2048]{1,0:T(8,128)(2,1)}, bf16[128,2048]{1,0:T(8,128)(2,1)}, u32[]{:S(2)}, u32[]{:S(2)}) collective-permute-start(bf16[128,2048]{1,0:T(8,128)(2,1)} %collective-permute-done.2.refs_4_.refs_8_), channel_id=1, source_target_pairs={{0,16},{16,0},{32,48},{48,32},{64,80},{80,64},{96,112},{112,96},{1... | collective-permute-start | bytes 1572872 | tf_op jit(solution)/shard_map/ppermute | solution.py:608
  46.0 28.0 %collective-permute-start.4 = (bf16[128,2048]{1,0:T(8,128)(2,1)}, bf16[128,2048]{1,0:T(8,128)(2,1)}, u32[]{:S(2)}, u32[]{:S(2)}) collective-permute-start(bf16[128,2048]{1,0:T(8,128)(2,1)} %collective-permute-done.1.refs_3_.refs_4_), channel_id=1, source_target_pairs={{0,16},{16,0},{32,48},{48,32},{64,80},{80,64},{96,112},{112,96},{1... | collective-permute-start | bytes 1572872 | tf_op jit(solution)/shard_map/ppermute | solution.py:608
  57.6 16.5 %collective-permute-start.5 = (bf16[128,2048]{1,0:T(8,128)(2,1)}, bf16[128,2048]{1,0:T(8,128)(2,1)}, u32[]{:S(2)}, u32[]{:S(2)}) collective-permute-start(bf16[128,2048]{1,0:T(8,128)(2,1)} %collective-permute-done.3.refs_7_.refs_6_), channel_id=1, source_target_pairs={{0,16},{16,0},{32,48},{48,32},{64,80},{80,64},{96,112},{112,96},{1... | collective-permute-start | bytes 1572872 | tf_op jit(solution)/shard_map/ppermute | solution.py:608
  62.2 14.8 %all-to-all-start.2 = ((bf16[16,128,128]{2,1,0:T(8,128)(2,1)}), bf16[16,128,128]{2,1,0:T(8,128)(2,1)}, u32[]{:S(2)}, u32[]{:S(2)}) async-start(bf16[16,128,128]{2,1,0:T(8,128)(2,1)} %get-tuple-element.20.refs_5_), calls=%async_computation.2 | async-start | bytes 1048576 | tf_op jit(solution)/shard_map/all_to_all | solution.py:603
